TPU v7x, 512 devices: a whole 4x4x16 slice. The times are simulated.
512 devices in a mesh: rep: 32 (over z, x_lo), fsdp: 16 (over y, x_hi, core).
Axes of the slice: x: 4 (x_hi: 2, x_lo: 2; x = x_hi * 2 + x_lo), y: 4, z: 16, core: 2. Of those that a mesh axis runs over, the one named last changes fastest.
Arguments:
- activations: bfloat16 [32, 3072, 4096], P('rep', 'fsdp'), may hold values from -6 to 6
- weights: float32 [32, 4096, 512], P('rep', 'fsdp'), may hold values from -6 to 6
- cotangent: bfloat16 [32, 3072, 512], P('rep', 'fsdp'), may hold values from -6 to 6
- step_index: int32 [1], replicated, may hold values from 0 to 999
Outputs:
- projected: bfloat16 [32, 3072, 512], P('rep', 'fsdp')
- input_grad: bfloat16 [32, 3072, 4096], P('rep', 'fsdp')
- mixed: float32 [32, 4096, 512], P('rep', 'fsdp')
All inputs are finite; a program needn't handle non-finite values.
Results may differ from a plain program's by a relative error of at most 0.005.
Values may be sent and summed in bfloat16 or wider, within the bound.
No kernel may reach another device: no remote copies, remote signals or barrier semaphores. Data moves between devices by JAX's collectives and lax.ppermute only.
A program may use at most 64 MiB of HBM per device.

v0:
```python
from functools import partial

import jax
import jax.numpy as jnp
from jax import lax
from jax.sharding import PartitionSpec as P

D = 4096
BITS = 3


def shortened(array):

    def short(part):
        return part.astype(jnp.bfloat16) if part.dtype == jnp.float32 else part

    return jax.tree.map(short, array)


def swapped(block, axis, apart):
    count = lax.axis_size(axis)
    route = []
    for low in range(count):
        high = low | 1 << apart
        if high != low and high < count:
            route += [(low, high), (high, low)]
    return lax.ppermute(block, axis, route)


def swap_with(bit_number, shard):
    return jax.tree.map(
        lambda part, own: part.astype(own.dtype),
        swapped(shortened(shard), "rep", bit_number),
        shard,
    )


def body(activations, weights, cotangent, step_index):
    inputs = activations[0]
    cotan = cotangent[0]
    master = weights[0]
    scale = D ** (-0.5)
    half_weights = master.astype(jnp.bfloat16)
    columns = inputs
    forward = jnp.dot(
        columns,
        lax.all_gather(half_weights, "fsdp", axis=0, tiled=True),
        preferred_element_type=jnp.float32,
    )
    backward = lax.dot_general(
        cotan,
        lax.all_gather(half_weights, "fsdp", axis=0, tiled=True),
        (((1,), (1,)), ((), ())),
        preferred_element_type=jnp.float32,
    )
    projected = (forward * scale).astype(jnp.bfloat16)
    input_grad = (backward * scale).astype(jnp.bfloat16)
    columns = inputs
    product = lax.dot_general(
        columns, cotan, (((0,), (0,)), ((), ())), preferred_element_type=jnp.float32
    )
    grad = lax.psum_scatter(
        (product * scale).astype(jnp.bfloat16), "fsdp", scatter_dimension=0, tiled=True
    ).astype(jnp.float32)
    rate = 0.3 / jnp.sqrt(1.0 + step_index[0].astype(jnp.float32) / 50.0)
    updated = master - rate * grad
    bit_index = step_index[0] % BITS
    branches = [partial(swap_with, number) for number in range(BITS)]
    other = lax.switch(bit_index, branches, updated)
    mixed = 0.5 * (updated + other)
    return (projected[None], input_grad[None], mixed[None])


def solution(mesh):
    return jax.shard_map(
        body,
        mesh=mesh,
        in_specs=(P("rep", "fsdp", None), P("rep", "fsdp", None), P("rep", "fsdp", None), P()),
        out_specs=(P("rep", "fsdp", None), P("rep", "fsdp", None), P("rep", "fsdp", None)),
        check_vma=False,
    )
```

profile of v0, /device:TPU:1, one launch (start us, length us, event | category | flops | bytes accessed | tf_op | source)
XLA Modules:
  0.0 209.8 jit_solution(14837117618580848214)
XLA Ops:
  7.2 0.0 copy-start
  7.2 0.0 reduce-scatter.2.cloned.1.call-start
  7.2 1.4 copy-done
  8.6 4.2 %multiply_convert_fusion = bf16[4096,512]{1,0:T(8,128)(2,1)} fusion(bf16[1,192,4096]{2,1,0:T(8,128)(2,1)S(1)} %copy-done, bf16[1,192,512]{2,1,0:T(8,128)(2,1)} %param.9), kind=kOutput, calls=%fused_computation | convolution fusion | flops 809500672 | bytes 5963776 | tf_op jit(solution)/shard_map/dot_general | solution.py:59
  12.8 0.0 copy-start.2
  12.8 0.0 reduce-scatter.2.cloned.1.call-update
  12.8 0.0 all-gather.2.cloned.1.call-start
  12.8 1.0 copy-done.2
  13.8 0.7 bitcast_convert_fusion
  14.6 0.0 all-gather.2.cloned.1.call-update
  15.3 105.2 %reduce-scatter.2.cloned.1.call-done = bf16[256,512]{1,0:T(8,128)(2,1)} async-done(((bf16[4096,512]{1,0:T(8,128)(2,1)}), bf16[256,512]{1,0:T(8,128)(2,1)}) %reduce-scatter.2.cloned.1.call-update) | async-done | bytes 262160 | tf_op jit(solution)/shard_map/reduce_scatter | solution.py:62
  120.5 1.0 bitcast_subtract_fusion
  121.5 7.7 %conditional.4 = (f32[256,512]{1,0:T(8,128)S(1)}) conditional(s32[]{:T(128)} %clamp.3, f32[256,512]{1,0:T(8,128)S(1)} %bitcast_subtract_fusion, f32[256,512]{1,0:T(8,128)S(1)} %bitcast_subtract_fusion, f32[256,512]{1,0:T(8,128)S(1)} %bitcast_subtract_fusion), branch_computations={%region_1.2_spmd, %region_2.3_spmd, %region_3.4_spmd} | conditional | flops 262144 | bytes 2621488
  121.6 2.2 %collective-permute-start = (bf16[256,512]{1,0:T(8,128)(2,1)S(1)}, bf16[256,512]{1,0:T(8,128)(2,1)S(1)}, u32[]{:S(2)}, u32[]{:S(2)}) collective-permute-start(bf16[256,512]{1,0:T(8,128)(2,1)S(1)} %convert_element_type.33), channel_id=1, source_target_pairs={{0,16},{16,0},{32,48},{48,32},{64,80},{80,64},{96,112},{112,96},{1... | collective-permute-start | bytes 786440 | tf_op jit(solution)/shard_map/cond/branch_0_fun/ppermute | solution.py:27
  123.8 5.4 %collective-permute-done = bf16[256,512]{1,0:T(8,128)(2,1)S(1)} collective-permute-done((bf16[256,512]{1,0:T(8,128)(2,1)S(1)}, bf16[256,512]{1,0:T(8,128)(2,1)S(1)}, u32[]{:S(2)}, u32[]{:S(2)}) %collective-permute-start) | collective-permute-done | bytes 262176 | tf_op jit(solution)/shard_map/cond/branch_0_fun/ppermute | solution.py:27
  129.2 0.0 copy-start.3
  129.2 0.9 multiply_bitcast_fusion
  130.1 66.2 %all-gather.2.cloned.1.call-done = bf16[4096,512]{1,0:T(8,128)(2,1)} async-done(((bf16[256,512]{1,0:T(8,128)(2,1)}), bf16[4096,512]{1,0:T(8,128)(2,1)}) %all-gather.2.cloned.1.call-update) | async-done | bytes 4194320 | tf_op jit(solution)/shard_map/all_gather | solution.py:47
  196.3 0.0 copy-start.1
  196.3 4.0 %fusion.11 = bf16[1,192,512]{2,1,0:T(8,128)(2,1)} fusion(bf16[4096,512]{1,0:T(8,128)(2,1)} %all-gather.2.cloned.1.call-done, bf16[1,192,4096]{2,1,0:T(8,128)(2,1)S(1)} %copy-done), kind=kOutput, calls=%fused_computation.9 | convolution fusion | flops 805502976 | bytes 5963776 | tf_op jit(solution)/shard_map/dot_general | solution.py:45
  200.3 0.0 copy-done.3
  200.3 0.0 copy-done.1
  200.3 2.7 %fusion.1 = bf16[1,192,4096]{2,1,0:T(8,128)(2,1)} fusion(bf16[4096,512]{1,0:T(8,128)(2,1)S(1)} %copy-done.1, bf16[1,192,512]{2,1,0:T(8,128)(2,1)S(1)} %copy-done.3), kind=kOutput, calls=%fused_computation.3 | convolution fusion | flops 806879232 | bytes 5963776 | tf_op jit(solution)/shard_map/dot_general | solution.py:50
  (2 shorter events, 0.1 us)
Async XLA Ops:
  7.2 1.4 copy-start
  7.2 113.3 %reduce-scatter.2.cloned.1.call-start = ((), (), s32[]{:S(2)}) async-start(), calls=%async_computation.2 | async-start | bytes 4456448 | tf_op jit(solution)/shard_map/reduce_scatter | solution.py:62
  12.8 1.0 copy-start.2
  12.8 183.5 %all-gather.2.cloned.1.call-start = ((), (), s32[]{:S(2)}) async-start(), calls=%async_computation.1 | async-start | bytes 4456448 | tf_op jit(solution)/shard_map/all_gather | solution.py:47
  121.6 7.6 %collective-permute-start = (bf16[256,512]{1,0:T(8,128)(2,1)S(1)}, bf16[256,512]{1,0:T(8,128)(2,1)S(1)}, u32[]{:S(2)}, u32[]{:S(2)}) collective-permute-start(bf16[256,512]{1,0:T(8,128)(2,1)S(1)} %convert_element_type.33), channel_id=1, source_target_pairs={{0,16},{16,0},{32,48},{48,32},{64,80},{80,64},{96,112},{112,96},{1... | collective-permute-start | bytes 786440 | tf_op jit(solution)/shard_map/cond/branch_0_fun/ppermute | solution.py:27
  129.2 71.1 %copy-start.3 = (bf16[1,192,512]{2,1,0:T(8,128)(2,1)S(1)}, bf16[1,192,512]{2,1,0:T(8,128)(2,1)}, u32[]{:S(2)}) copy-start(bf16[1,192,512]{2,1,0:T(8,128)(2,1)} %param.9) | copy-start | bytes 589828
  196.3 4.0 %copy-start.1 = (bf16[4096,512]{1,0:T(8,128)(2,1)S(1)}, bf16[4096,512]{1,0:T(8,128)(2,1)}, u32[]{:S(2)}) copy-start(bf16[4096,512]{1,0:T(8,128)(2,1)} %all-gather.2.cloned.1.call-done) | copy-start | bytes 12582916
Sparse Core Ops, SparseCore 0:
  12.9 107.5 reduce-scatter.1
  124.9 71.3 all-gather.1
where the time goes:
time: 210 us
  waiting for transfers between devices  177 us (84%)
  between operations  14.8 us (7%)
  matrix products  10.8 us (5%)
  other arithmetic  2.72 us (1%)
  local copies, waits for them, and re-layouts  2.34 us (1%)
  starting transfers between devices  2.29 us (1%)
    reduce_scatter x1, waiting for transfers between devices, body(): lax.psum_scatter((product * scale).astype(jnp.bfloat16), 'fsdp', scatter_...  105 us
    all_gather x1, waiting for transfers between devices, body(): lax.all_gather(half_weights, 'fsdp', axis=0, tiled=True)  66.2 us
    ppermute x1, waiting for transfers between devices, swapped(): return lax.ppermute(block, axis, route)  5.36 us
  transfers between devices with their start and end apart: 3, of which 3 were waited for; matrix products, arithmetic and copies ran while one was open for 1% of the time, Pallas kernels for 0%

commit v1 on v0

v1 whole, which is shorter than its diff:
```python
from functools import partial

import jax
import jax.numpy as jnp
from jax import lax
from jax.experimental import pallas as pl
from jax.experimental.pallas import tpu as pltpu
from jax.sharding import PartitionSpec as P

D = 4096
KW = 512
BITS = 3
CORES = 2
SPAN = 2
RINGS = 4
SIDES = CORES * SPAN
ROWS = D // (SIDES * RINGS)
SCALE = D ** (-0.5)
ALONG_Y = [[side + SIDES * y for y in range(RINGS)] for side in range(SIDES)]
IN_VMEM = pl.BlockSpec(memory_space=pltpu.VMEM)
IN_SMEM = pl.BlockSpec(memory_space=pltpu.SMEM)
PARAMS = pltpu.CompilerParams(vmem_limit_bytes=16 << 20)


def swapped(block, axis, apart):
    count = lax.axis_size(axis)
    return lax.ppermute(block, axis, [(low, low ^ apart) for low in range(count)])


def along_y(block):
    return lax.all_to_all(block, "fsdp", 0, 0, tiled=True, axis_index_groups=ALONG_Y)


def shifted(block, hops):
    count = SIDES * RINGS
    return lax.ppermute(block, "fsdp", [(place, (place + SIDES * hops) % count) for place in range(count)])


def after(value, earlier):
    return lax.optimization_barrier((value, earlier))[0]


def columns(block):
    return pl.ds(pl.multiple_of(block * ROWS, ROWS), ROWS)


def terms_kernel(spot, inputs, partner_inputs, cotan, partner_cotan, kept, given):
    turned = cotan[...].T
    partner_turned = partner_cotan[...].T
    for out, side in ((kept, spot[1]), (given, 1 - spot[1])):
        for y in range(RINGS):
            at = columns(SIDES * y + CORES * side + spot[0])
            total = jnp.dot(turned, inputs[:, at], preferred_element_type=jnp.float32)
            total += jnp.dot(partner_turned, partner_inputs[:, at], preferred_element_type=jnp.float32)
            out[y] = (total * SCALE).astype(jnp.bfloat16)


def terms_of(spot, inputs, partner_inputs, cotan, partner_cotan):
    return pl.pallas_call(
        terms_kernel,
        in_specs=[IN_SMEM] + [IN_VMEM] * 4,
        out_specs=[IN_VMEM] * 2,
        out_shape=[jax.ShapeDtypeStruct((RINGS, KW, ROWS), jnp.bfloat16)] * 2,
        compiler_params=PARAMS,
        cost_estimate=pl.CostEstimate(flops=inputs.size, bytes_accessed=1 << 20, transcendentals=0),
        name="gradient_terms",
    )(spot, inputs, partner_inputs, cotan, partner_cotan)


def copies_kernel(master, near, out):
    for y in range(RINGS):
        out[y, 0] = master[...].astype(jnp.bfloat16)
        out[y, 1] = near[...]


def copies_of(master, near):
    return pl.pallas_call(
        copies_kernel,
        in_specs=[IN_VMEM] * 2,
        out_specs=IN_VMEM,
        out_shape=jax.ShapeDtypeStruct((RINGS, SPAN, ROWS, KW), jnp.bfloat16),
        compiler_params=PARAMS,
        cost_estimate=pl.CostEstimate(flops=1 << 38, bytes_accessed=3 << 20, transcendentals=0),
        name="copies",
    )(master, near)


def fold_kernel(spot, kept, taken, *sent):
    for hops, out in zip((1, 2, 3), sent):
        y = lax.rem(spot[2] + hops, RINGS)
        out[...] = (kept[y].astype(jnp.float32) + taken[y].astype(jnp.float32)).astype(jnp.bfloat16)


def fold_of(spot, kept, taken):
    return pl.pallas_call(
        fold_kernel,
        in_specs=[IN_SMEM] + [IN_VMEM] * 2,
        out_specs=[IN_VMEM] * (RINGS - 1),
        out_shape=[jax.ShapeDtypeStruct((KW, ROWS), jnp.bfloat16)] * (RINGS - 1),
        compiler_params=PARAMS,
        cost_estimate=pl.CostEstimate(flops=1 << 38, bytes_accessed=3 << 20, transcendentals=0),
        name="fold",
    )(spot, kept, taken)


def own_kernel(spot, kept, taken, own):
    own[...] = kept[spot[2]].astype(jnp.float32) + taken[spot[2]].astype(jnp.float32)


def own_of(spot, kept, taken):
    return pl.pallas_call(
        own_kernel,
        in_specs=[IN_SMEM] + [IN_VMEM] * 2,
        out_specs=IN_VMEM,
        out_shape=jax.ShapeDtypeStruct((KW, ROWS), jnp.float32),
        compiler_params=PARAMS,
        cost_estimate=pl.CostEstimate(flops=1 << 38, bytes_accessed=3 << 20, transcendentals=0),
        name="fold_own",
    )(spot, kept, taken)


def update_kernel(rate, master, own, first, second, third, updated, short):
    grad = (own[...] + first[...].astype(jnp.float32)) + (
        second[...].astype(jnp.float32) + third[...].astype(jnp.float32)
    )
    new = master[...] - rate[0] * grad.T
    updated[...] = new
    short[...] = new.astype(jnp.bfloat16)


def update_of(rate, master, *parts):
    return pl.pallas_call(
        update_kernel,
        in_specs=[IN_SMEM] + [IN_VMEM] * 5,
        out_specs=[IN_VMEM] * 2,
        out_shape=[
            jax.ShapeDtypeStruct((ROWS, KW), jnp.float32),
            jax.ShapeDtypeStruct((ROWS, KW), jnp.bfloat16),
        ],
        compiler_params=PARAMS,
        cost_estimate=pl.CostEstimate(flops=8 * ROWS * KW, bytes_accessed=2 << 20, transcendentals=0),
        name="update",
    )(rate, master, *parts)


def mix_kernel(updated, other, mixed):
    mixed[...] = 0.5 * (updated[...] + other[...].astype(jnp.float32))


def mix_of(updated, other):
    return pl.pallas_call(
        mix_kernel,
        in_specs=[IN_VMEM] * 2,
        out_specs=IN_VMEM,
        out_shape=jax.ShapeDtypeStruct((ROWS, KW), jnp.float32),
        compiler_params=PARAMS,
        cost_estimate=pl.CostEstimate(flops=2 * ROWS * KW, bytes_accessed=2 << 20, transcendentals=0),
        name="mix",
    )(updated, other)


def keys_kernel(spot, inputs, cotan, mine, theirs, forward, backward, total):
    core, across = spot[0], spot[1]
    over_width = (((1,), (1,)), ((), ()))
    for y in range(RINGS):
        for side in range(SPAN):
            for rows, whose in ((mine, core), (theirs, 1 - core)):
                at = columns(SIDES * y + CORES * (across ^ side) + whose)
                part = rows[y, side]
                product = jnp.dot(inputs[:, at], part, preferred_element_type=jnp.float32)
                if y == 0 and side == 0 and rows is mine:
                    total[...] = product
                else:
                    total[...] += product
                back = lax.dot_general(cotan[...], part, over_width, preferred_element_type=jnp.float32)
                backward[:, at] = (back * SCALE).astype(jnp.bfloat16)
    forward[...] = (total[...] * SCALE).astype(jnp.bfloat16)


def keys_of(spot, inputs, cotan, mine, theirs):
    tokens = inputs.shape[0]
    return pl.pallas_call(
        keys_kernel,
        in_specs=[IN_SMEM] + [IN_VMEM] * 4,
        out_specs=[IN_VMEM] * 2,
        scratch_shapes=[pltpu.VMEM((tokens, KW), jnp.float32)],
        out_shape=[
            jax.ShapeDtypeStruct((tokens, KW), jnp.bfloat16),
            jax.ShapeDtypeStruct((tokens, D), jnp.bfloat16),
        ],
        compiler_params=PARAMS,
        cost_estimate=pl.CostEstimate(flops=tokens * D, bytes_accessed=1 << 20, transcendentals=0),
        name="keys_and_input_gradient",
    )(spot, inputs, cotan, mine, theirs)


def step(bit, inputs, master, cotan, rate):
    place = lax.axis_index("fsdp")
    spot = jnp.stack((place % CORES, place // CORES % SPAN, place // SIDES)).astype(jnp.int32)

    near_weights = swapped(master.astype(jnp.bfloat16), "fsdp", CORES)
    tokens = (inputs, swapped(inputs, "fsdp", 1), cotan, swapped(cotan, "fsdp", 1))
    kept, given = terms_of(spot, *tokens)
    taken = swapped(given, "fsdp", CORES)

    mine = along_y(copies_of(master, after(near_weights, given)))

    sent = fold_of(spot, kept, taken)
    own = own_of(spot, kept, after(taken, sent[0]))
    arrived = [shifted(part, hops) for hops, part in zip((1, 2, 3), sent)]
    theirs = swapped(after(mine, sent[0]), "fsdp", 1)
    updated, short = update_of(rate[None], master, own, *arrived)
    other = swapped(short, "rep", 1 << bit)
    projected, input_grad = keys_of(spot, inputs, cotan, mine, theirs)
    mixed = mix_of(updated, after(other, projected))
    return (projected[None], input_grad[None], mixed[None])


def body(activations, weights, cotangent, step_index):
    rate = 0.3 / jnp.sqrt(1.0 + step_index[0].astype(jnp.float32) / 50.0)
    branches = [partial(step, bit) for bit in range(BITS)]
    return lax.switch(step_index[0] % BITS, branches, activations[0], weights[0], cotangent[0], rate)


def solution(mesh):
    return jax.shard_map(
        body,
        mesh=mesh,
        in_specs=(P("rep", "fsdp", None), P("rep", "fsdp", None), P("rep", "fsdp", None), P()),
        out_specs=(P("rep", "fsdp", None), P("rep", "fsdp", None), P("rep", "fsdp", None)),
        check_vma=False,
    )
```

time: 210 us -> 82.3 us (0.39)
  the two profiles are of different devices: /device:TPU:1 before, /device:TPU:28 now
where the time goes in v1:
time: 82.3 us; the launch traced here: 81.7 us
  starting transfers between devices  34.7 us (42%)
  waiting for transfers between devices  26.6 us (32%)
  Pallas kernels  17.6 us (21%)
  between operations  1.3 us (2%)
  other arithmetic  1.15 us (1%)
    ppermute x6, waiting for transfers between devices, swapped(): lax.ppermute(block, axis, [(low, low ^ apart) for low in range(count)])  18 us
    ppermute x6, starting transfers between devices, swapped(): lax.ppermute(block, axis, [(low, low ^ apart) for low in range(count)])  15.2 us
    ppermute x3, starting transfers between devices, shifted(): lax.ppermute(block, 'fsdp', [(place, (place + SIDES * hops) % count) for...  12.2 us
    ppermute x3, waiting for transfers between devices, shifted(): lax.ppermute(block, 'fsdp', [(place, (place + SIDES * hops) % count) for...  8.63 us
    all_to_all x1, starting transfers between devices, along_y(): lax.all_to_all(block, 'fsdp', 0, 0, tiled=True, axis_index_groups=ALONG_Y)  7.28 us
    pallas_call x1, Pallas kernels, keys_of(): pl.pallas_call(keys_kernel, in_specs=[IN_SMEM] + [IN_VMEM] * 4, out_specs...  5.61 us
    pallas_call x1, Pallas kernels, terms_of(): pl.pallas_call(terms_kernel, in_specs=[IN_SMEM] + [IN_VMEM] * 4, out_spec...  3.68 us
    pallas_call x1, Pallas kernels, copies_of(): pl.pallas_call(copies_kernel, in_specs=[IN_VMEM] * 2, out_specs=IN_VMEM,...  2.55 us
  transfers between devices with their start and end apart: 10, of which 5 were waited for; matrix products, arithmetic and copies ran while one was open for 1% of the time, Pallas kernels for 21%

profile of v1, /device:TPU:28, one launch (start us, length us, event | category | flops | bytes accessed | tf_op | source)
XLA Modules:
  0.0 81.7 jit_solution(4693027441423479067)
XLA Ops:
  1.3 80.4 %conditional.1 = (bf16[1,192,512]{2,1,0:T(8,128)(2,1)}, bf16[1,192,4096]{2,1,0:T(8,128)(2,1)}, f32[1,256,512]{2,1,0:T(8,128)}) conditional(s32[]{:T(128)} %clamp.3, (f32[1,256,512]{2,1,0:T(8,128)}, bf16[1,192,4096]{2,1,0:T(8,128)(2,1)}, bf16[1,192,512]{2,1,0:T(8,128)(2,1)}, (), f32[1]{0:T(128)}, /*index=5*/(), ()) %tuple.31, ...), branch_computations={%region_0.1_spmd, %region_1.2_spmd, %region_2.3_spmd} | conditional | flops 824636735488 | bytes 56886388 | solution.py:222
  1.3 1.9 %collective-permute-start.10 = (bf16[192,4096]{1,0:T(8,128)(2,1)}, bf16[192,4096]{1,0:T(8,128)(2,1)S(1)}, u32[]{:S(2)}, u32[]{:S(2)}) collective-permute-start(bf16[192,4096]{1,0:T(8,128)(2,1)} %bitcast.34), channel_id=1, source_target_pairs={{0,1},{1,0},{2,3},{3,2},{4,5},{5,4},{6,7},{7,6},{8,9},{9,8},{10,11... | collective-permute-start | bytes 4718600 | tf_op jit(solution)/shard_map/cond/branch_1_fun/ppermute | solution.py:27
  3.2 1.1 %bitcast_convert_fusion.1 = bf16[256,512]{1,0:T(8,128)(2,1)S(1)} fusion(f32[1,256,512]{2,1,0:T(8,128)} %get-tuple-element.109), kind=kLoop, calls=%fused_computation.3 | loop fusion | flops 131072 | bytes 786432 | tf_op jit(solution)/shard_map/cond/branch_1_fun/convert_element_type | solution.py:201
  4.3 2.4 %collective-permute-start.9 = (bf16[256,512]{1,0:T(8,128)(2,1)S(1)}, bf16[256,512]{1,0:T(8,128)(2,1)S(1)}, u32[]{:S(2)}, u32[]{:S(2)}) collective-permute-start(bf16[256,512]{1,0:T(8,128)(2,1)S(1)} %bitcast_convert_fusion.1), channel_id=1, source_target_pairs={{0,2},{1,3},{2,0},{3,1},{4,6},{5,7},{6,4},{7,5},{8,10},{9,11},{10,... | collective-permute-start | bytes 786440 | tf_op jit(solution)/shard_map/cond/branch_1_fun/ppermute | solution.py:27
  6.8 2.1 %collective-permute-start.11 = (bf16[192,512]{1,0:T(8,128)(2,1)}, bf16[192,512]{1,0:T(8,128)(2,1)S(1)}, u32[]{:S(2)}, u32[]{:S(2)}) collective-permute-start(bf16[192,512]{1,0:T(8,128)(2,1)} %bitcast.49), channel_id=1, source_target_pairs={{0,1},{1,0},{2,3},{3,2},{4,5},{5,4},{6,7},{7,6},{8,9},{9,8},{10,11... | collective-permute-start | bytes 589832 | tf_op jit(solution)/shard_map/cond/branch_1_fun/ppermute | solution.py:27
  9.1 1.2 %collective-permute-done.11.partner_cotan = bf16[192,512]{1,0:T(8,128)(2,1)S(1)} collective-permute-done((bf16[192,512]{1,0:T(8,128)(2,1)}, bf16[192,512]{1,0:T(8,128)(2,1)S(1)}, u32[]{:S(2)}, u32[]{:S(2)}) %collective-permute-start.11) | collective-permute-done | bytes 196640 | tf_op jit(solution)/shard_map/cond/branch_1_fun/ppermute | solution.py:27
  10.3 3.7 %gradient_terms.4 = (bf16[4,512,256]{2,1,0:T(8,128)(2,1)S(1)}, bf16[4,512,256]{2,1,0:T(8,128)(2,1)}) custom-call(s32[3]{0:T(128)S(1)} %pad_add_fusion.1.spot, bf16[192,4096]{1,0:T(8,128)(2,1)} %bitcast.35, bf16[192,4096]{1,0:T(8,128)(2,1)S(1)} %collective-permute-done.10.partner_inputs, bf16[192,512]{1,0:T(8,128)(2,1)} %bitcast.50, ...), custom_call_target="tpu_custom_call" | custom-call | flops 786432 | bytes 1048576 | tf_op jit(solution)/shard_map/cond/branch_1_fun/gradient_terms/pallas_call | solution.py:59
  14.0 4.9 %collective-permute-start.12 = (bf16[4,512,256]{2,1,0:T(8,128)(2,1)}, bf16[4,512,256]{2,1,0:T(8,128)(2,1)}, u32[]{:S(2)}, u32[]{:S(2)}) collective-permute-start(bf16[4,512,256]{2,1,0:T(8,128)(2,1)} %get-tuple-element.44), channel_id=1, source_target_pairs={{0,2},{1,3},{2,0},{3,1},{4,6},{5,7},{6,4},{7,5},{8,10},{9,11},{10,... | collective-permute-start | bytes 3145736 | tf_op jit(solution)/shard_map/cond/branch_1_fun/ppermute | solution.py:27
  18.9 2.6 %copies.4 = bf16[4,2,256,512]{3,2,1,0:T(8,128)(2,1)} custom-call(f32[256,512]{1,0:T(8,128)} %bitcast.42, bf16[256,512]{1,0:T(8,128)(2,1)S(1)} %collective-permute-done.9.near), custom_call_target="tpu_custom_call" | custom-call | flops 274877906944 | bytes 3145728 | tf_op jit(solution)/shard_map/cond/branch_1_fun/copies/pallas_call | solution.py:77
  21.5 7.3 %all-to-all-start.1 = ((bf16[4,2,256,512]{3,2,1,0:T(8,128)(2,1)}), bf16[4,2,256,512]{3,2,1,0:T(8,128)(2,1)}, u32[]{:S(2)}, u32[]{:S(2)}) async-start(bf16[4,2,256,512]{3,2,1,0:T(8,128)(2,1)} %copies.4), calls=%async_computation.1 | async-start | bytes 4194304 | tf_op jit(solution)/shard_map/cond/branch_1_fun/all_to_all | solution.py:31
  28.8 14.2 %collective-permute-done.12.taken = bf16[4,512,256]{2,1,0:T(8,128)(2,1)} collective-permute-done((bf16[4,512,256]{2,1,0:T(8,128)(2,1)}, bf16[4,512,256]{2,1,0:T(8,128)(2,1)}, u32[]{:S(2)}, u32[]{:S(2)}) %collective-permute-start.12) | collective-permute-done | bytes 1048608 | tf_op jit(solution)/shard_map/cond/branch_1_fun/ppermute | solution.py:27
  43.0 2.2 %fold.4 = (bf16[512,256]{1,0:T(8,128)(2,1)}, bf16[512,256]{1,0:T(8,128)(2,1)}, bf16[512,256]{1,0:T(8,128)(2,1)}) custom-call(s32[3]{0:T(128)S(1)} %copy-done.3, bf16[4,512,256]{2,1,0:T(8,128)(2,1)S(1)} %get-tuple-element.46.kept, bf16[4,512,256]{2,1,0:T(8,128)(2,1)} %collective-permute-done.12.taken), custom_call_target="tpu_custom_call" | custom-call | flops 274877906944 | bytes 3145728 | tf_op jit(solution)/shard_map/cond/branch_1_fun/fold/pallas_call | solution.py:95
  45.2 7.5 %collective-permute-start.14 = (bf16[512,256]{1,0:T(8,128)(2,1)}, bf16[512,256]{1,0:T(8,128)(2,1)}, u32[]{:S(2)}, u32[]{:S(2)}) collective-permute-start(bf16[512,256]{1,0:T(8,128)(2,1)} %get-tuple-element.47), channel_id=1, source_target_pairs={{0,4},{1,5},{2,6},{3,7},{4,8},{5,9},{6,10},{7,11},{8,12},{9,13},{1... | collective-permute-start | bytes 786440 | tf_op jit(solution)/shard_map/cond/branch_1_fun/ppermute | solution.py:36
  52.7 1.9 %collective-permute-start.15 = (bf16[512,256]{1,0:T(8,128)(2,1)}, bf16[512,256]{1,0:T(8,128)(2,1)}, u32[]{:S(2)}, u32[]{:S(2)}) collective-permute-start(bf16[512,256]{1,0:T(8,128)(2,1)} %get-tuple-element.53), channel_id=1, source_target_pairs={{0,8},{1,9},{2,10},{3,11},{4,12},{5,13},{6,14},{7,15},{8,0},{9,1},... | collective-permute-start | bytes 786440 | tf_op jit(solution)/shard_map/cond/branch_1_fun/ppermute | solution.py:36
  54.6 2.8 %collective-permute-start.16 = (bf16[512,256]{1,0:T(8,128)(2,1)}, bf16[512,256]{1,0:T(8,128)(2,1)}, u32[]{:S(2)}, u32[]{:S(2)}) collective-permute-start(bf16[512,256]{1,0:T(8,128)(2,1)} %get-tuple-element.54), channel_id=1, source_target_pairs={{0,12},{1,13},{2,14},{3,15},{4,0},{5,1},{6,2},{7,3},{8,4},{9,5},{1... | collective-permute-start | bytes 786440 | tf_op jit(solution)/shard_map/cond/branch_1_fun/ppermute | solution.py:36
  57.4 1.9 %collective-permute-start.13 = (bf16[4,2,256,512]{3,2,1,0:T(8,128)(2,1)}, bf16[4,2,256,512]{3,2,1,0:T(8,128)(2,1)}, u32[]{:S(2)}, u32[]{:S(2)}) collective-permute-start(bf16[4,2,256,512]{3,2,1,0:T(8,128)(2,1)} %all-to-all-done.1.mine), channel_id=1, source_target_pairs={{0,1},{1,0},{2,3},{3,2},{4,5},{5,4},{6,7},{7,6},{8,9},{9,8},{10,11... | collective-permute-start | bytes 6291464 | tf_op jit(solution)/shard_map/cond/branch_1_fun/ppermute | solution.py:27
  59.4 1.4 %fold_own.4.own = f32[512,256]{1,0:T(8,128)S(1)} custom-call(s32[3]{0:T(128)S(1)} %copy-done.3, bf16[4,512,256]{2,1,0:T(8,128)(2,1)S(1)} %get-tuple-element.46.kept, bf16[4,512,256]{2,1,0:T(8,128)(2,1)} %collective-permute-done.12.taken), custom_call_target="tpu_custom_call" | custom-call | flops 274877906944 | bytes 3145728 | tf_op jit(solution)/shard_map/cond/branch_1_fun/fold_own/pallas_call | solution.py:111
  60.7 5.0 %collective-permute-done.15.second = bf16[512,256]{1,0:T(8,128)(2,1)} collective-permute-done((bf16[512,256]{1,0:T(8,128)(2,1)}, bf16[512,256]{1,0:T(8,128)(2,1)}, u32[]{:S(2)}, u32[]{:S(2)}) %collective-permute-start.15) | collective-permute-done | bytes 262176 | tf_op jit(solution)/shard_map/cond/branch_1_fun/ppermute | solution.py:36
  65.7 3.7 %collective-permute-done.16.third = bf16[512,256]{1,0:T(8,128)(2,1)} collective-permute-done((bf16[512,256]{1,0:T(8,128)(2,1)}, bf16[512,256]{1,0:T(8,128)(2,1)}, u32[]{:S(2)}, u32[]{:S(2)}) %collective-permute-start.16) | collective-permute-done | bytes 262176 | tf_op jit(solution)/shard_map/cond/branch_1_fun/ppermute | solution.py:36
  69.4 1.3 %update.4 = (f32[256,512]{1,0:T(8,128)S(1)}, bf16[256,512]{1,0:T(8,128)(2,1)S(1)}) custom-call(f32[1]{0:T(128)S(6)} %div.58.rate, f32[256,512]{1,0:T(8,128)S(1)} %bitcast.43, f32[512,256]{1,0:T(8,128)S(1)} %fold_own.4.own, bf16[512,256]{1,0:T(8,128)(2,1)} %collective-permute-done.14.first, bf16[512,256]{1,0:T(8,128)(2,1)} %collective-permute-done.15.second, ...), custom_call_target="tpu_custom_call" | custom-call | flops 1048576 | bytes 2097152 | tf_op jit(solution)/shard_map/cond/branch_1_fun/update/pallas_call | solution.py:132
  70.7 1.9 %collective-permute-start.17 = (bf16[256,512]{1,0:T(8,128)(2,1)S(1)}, bf16[256,512]{1,0:T(8,128)(2,1)S(1)}, u32[]{:S(2)}, u32[]{:S(2)}) collective-permute-start(bf16[256,512]{1,0:T(8,128)(2,1)S(1)} %get-tuple-element.56), channel_id=1, source_target_pairs={{0,32},{16,48},{32,0},{48,16},{64,96},{80,112},{96,64},{112,80},{1... | collective-permute-start | bytes 786440 | tf_op jit(solution)/shard_map/cond/branch_1_fun/ppermute | solution.py:27
  72.7 5.6 %keys_and_input_gradient.4 = (bf16[192,512]{1,0:T(8,128)(2,1)}, bf16[192,4096]{1,0:T(8,128)(2,1)}) custom-call(s32[3]{0:T(128)S(1)} %copy-done.3, bf16[192,4096]{1,0:T(8,128)(2,1)S(1)} %bitcast.36, bf16[192,512]{1,0:T(8,128)(2,1)S(1)} %bitcast.51, bf16[4,2,256,512]{3,2,1,0:T(8,128)(2,1)} %all-to-all-done.1.mine, ...), custom_call_target="tpu_custom_call" | custom-call | flops 786432 | bytes 1048576 | tf_op jit(solution)/shard_map/cond/branch_1_fun/keys_and_input_gradient/pallas_call | solution.py:182
  78.3 2.6 %collective-permute-done.17.other = bf16[256,512]{1,0:T(8,128)(2,1)S(1)} collective-permute-done((bf16[256,512]{1,0:T(8,128)(2,1)S(1)}, bf16[256,512]{1,0:T(8,128)(2,1)S(1)}, u32[]{:S(2)}, u32[]{:S(2)}) %collective-permute-start.17) | collective-permute-done | bytes 262176 | tf_op jit(solution)/shard_map/cond/branch_1_fun/ppermute | solution.py:27
  80.8 0.8 %mix.4 = f32[256,512]{1,0:T(8,128)} custom-call(f32[256,512]{1,0:T(8,128)S(1)} %get-tuple-element.55.updated, bf16[256,512]{1,0:T(8,128)(2,1)S(1)} %collective-permute-done.17.other), custom_call_target="tpu_custom_call" | custom-call | flops 262144 | bytes 2097152 | tf_op jit(solution)/shard_map/cond/branch_1_fun/mix/pallas_call | solution.py:151
  (16 shorter events, 0.1 us)
Async XLA Ops:
  1.3 9.0 %collective-permute-start.10 = (bf16[192,4096]{1,0:T(8,128)(2,1)}, bf16[192,4096]{1,0:T(8,128)(2,1)S(1)}, u32[]{:S(2)}, u32[]{:S(2)}) collective-permute-start(bf16[192,4096]{1,0:T(8,128)(2,1)} %bitcast.34), channel_id=1, source_target_pairs={{0,1},{1,0},{2,3},{3,2},{4,5},{5,4},{6,7},{7,6},{8,9},{9,8},{10,11... | collective-permute-start | bytes 4718600 | tf_op jit(solution)/shard_map/cond/branch_1_fun/ppermute | solution.py:27
  4.3 14.6 %collective-permute-start.9 = (bf16[256,512]{1,0:T(8,128)(2,1)S(1)}, bf16[256,512]{1,0:T(8,128)(2,1)S(1)}, u32[]{:S(2)}, u32[]{:S(2)}) collective-permute-start(bf16[256,512]{1,0:T(8,128)(2,1)S(1)} %bitcast_convert_fusion.1), channel_id=1, source_target_pairs={{0,2},{1,3},{2,0},{3,1},{4,6},{5,7},{6,4},{7,5},{8,10},{9,11},{10,... | collective-permute-start | bytes 786440 | tf_op jit(solution)/shard_map/cond/branch_1_fun/ppermute | solution.py:27
  6.8 3.5 %collective-permute-start.11 = (bf16[192,512]{1,0:T(8,128)(2,1)}, bf16[192,512]{1,0:T(8,128)(2,1)S(1)}, u32[]{:S(2)}, u32[]{:S(2)}) collective-permute-start(bf16[192,512]{1,0:T(8,128)(2,1)} %bitcast.49), channel_id=1, source_target_pairs={{0,1},{1,0},{2,3},{3,2},{4,5},{5,4},{6,7},{7,6},{8,9},{9,8},{10,11... | collective-permute-start | bytes 589832 | tf_op jit(solution)/shard_map/cond/branch_1_fun/ppermute | solution.py:27
  9.1 4.9 %copy-start.2 = (s32[3]{0:T(128)}, s32[3]{0:T(128)S(1)}, u32[]{:S(2)}) copy-start(s32[3]{0:T(128)S(1)} %pad_add_fusion.1.spot) | copy-start | bytes 40 | tf_op jit(solution)/shard_map/cond
  14.0 29.0 %collective-permute-start.12 = (bf16[4,512,256]{2,1,0:T(8,128)(2,1)}, bf16[4,512,256]{2,1,0:T(8,128)(2,1)}, u32[]{:S(2)}, u32[]{:S(2)}) collective-permute-start(bf16[4,512,256]{2,1,0:T(8,128)(2,1)} %get-tuple-element.44), channel_id=1, source_target_pairs={{0,2},{1,3},{2,0},{3,1},{4,6},{5,7},{6,4},{7,5},{8,10},{9,11},{10,... | collective-permute-start | bytes 3145736 | tf_op jit(solution)/shard_map/cond/branch_1_fun/ppermute | solution.py:27
  21.5 21.5 %copy-start.3 = (s32[3]{0:T(128)S(1)}, s32[3]{0:T(128)}, u32[]{:S(2)}) copy-start(s32[3]{0:T(128)} %copy-done.2) | copy-start | bytes 40 | tf_op jit(solution)/shard_map/cond
  21.5 35.9 %all-to-all-start.1 = ((bf16[4,2,256,512]{3,2,1,0:T(8,128)(2,1)}), bf16[4,2,256,512]{3,2,1,0:T(8,128)(2,1)}, u32[]{:S(2)}, u32[]{:S(2)}) async-start(bf16[4,2,256,512]{3,2,1,0:T(8,128)(2,1)} %copies.4), calls=%async_computation.1 | async-start | bytes 4194304 | tf_op jit(solution)/shard_map/cond/branch_1_fun/all_to_all | solution.py:31
  45.2 24.2 %collective-permute-start.14 = (bf16[512,256]{1,0:T(8,128)(2,1)}, bf16[512,256]{1,0:T(8,128)(2,1)}, u32[]{:S(2)}, u32[]{:S(2)}) collective-permute-start(bf16[512,256]{1,0:T(8,128)(2,1)} %get-tuple-element.47), channel_id=1, source_target_pairs={{0,4},{1,5},{2,6},{3,7},{4,8},{5,9},{6,10},{7,11},{8,12},{9,13},{1... | collective-permute-start | bytes 786440 | tf_op jit(solution)/shard_map/cond/branch_1_fun/ppermute | solution.py:36
  52.7 13.0 %collective-permute-start.15 = (bf16[512,256]{1,0:T(8,128)(2,1)}, bf16[512,256]{1,0:T(8,128)(2,1)}, u32[]{:S(2)}, u32[]{:S(2)}) collective-permute-start(bf16[512,256]{1,0:T(8,128)(2,1)} %get-tuple-element.53), channel_id=1, source_target_pairs={{0,8},{1,9},{2,10},{3,11},{4,12},{5,13},{6,14},{7,15},{8,0},{9,1},... | collective-permute-start | bytes 786440 | tf_op jit(solution)/shard_map/cond/branch_1_fun/ppermute | solution.py:36
  54.6 14.7 %collective-permute-start.16 = (bf16[512,256]{1,0:T(8,128)(2,1)}, bf16[512,256]{1,0:T(8,128)(2,1)}, u32[]{:S(2)}, u32[]{:S(2)}) collective-permute-start(bf16[512,256]{1,0:T(8,128)(2,1)} %get-tuple-element.54), channel_id=1, source_target_pairs={{0,12},{1,13},{2,14},{3,15},{4,0},{5,1},{6,2},{7,3},{8,4},{9,5},{1... | collective-permute-start | bytes 786440 | tf_op jit(solution)/shard_map/cond/branch_1_fun/ppermute | solution.py:36
  57.4 15.2 %collective-permute-start.13 = (bf16[4,2,256,512]{3,2,1,0:T(8,128)(2,1)}, bf16[4,2,256,512]{3,2,1,0:T(8,128)(2,1)}, u32[]{:S(2)}, u32[]{:S(2)}) collective-permute-start(bf16[4,2,256,512]{3,2,1,0:T(8,128)(2,1)} %all-to-all-done.1.mine), channel_id=1, source_target_pairs={{0,1},{1,0},{2,3},{3,2},{4,5},{5,4},{6,7},{7,6},{8,9},{9,8},{10,11... | collective-permute-start | bytes 6291464 | tf_op jit(solution)/shard_map/cond/branch_1_fun/ppermute | solution.py:27
  59.3 10.0 %copy-start.10 = (f32[1,256,512]{2,1,0:T(8,128)S(1)}, f32[1,256,512]{2,1,0:T(8,128)}, u32[]{:S(2)}) copy-start(f32[1,256,512]{2,1,0:T(8,128)} %get-tuple-element.109) | copy-start | bytes 1572868 | tf_op jit(solution)/shard_map/cond
  59.4 13.3 %copy-start.13 = (bf16[1,192,512]{2,1,0:T(8,128)(2,1)S(1)}, bf16[1,192,512]{2,1,0:T(8,128)(2,1)}, u32[]{:S(2)}) copy-start(bf16[1,192,512]{2,1,0:T(8,128)(2,1)} %get-tuple-element.115) | copy-start | bytes 589828 | tf_op jit(solution)/shard_map/cond
  60.7 11.9 %copy-start.7 = (bf16[1,192,4096]{2,1,0:T(8,128)(2,1)S(1)}, bf16[1,192,4096]{2,1,0:T(8,128)(2,1)}, u32[]{:S(2)}) copy-start(bf16[1,192,4096]{2,1,0:T(8,128)(2,1)} %get-tuple-element.112) | copy-start | bytes 4718596 | tf_op jit(solution)/shard_map/cond
  70.7 10.1 %collective-permute-start.17 = (bf16[256,512]{1,0:T(8,128)(2,1)S(1)}, bf16[256,512]{1,0:T(8,128)(2,1)S(1)}, u32[]{:S(2)}, u32[]{:S(2)}) collective-permute-start(bf16[256,512]{1,0:T(8,128)(2,1)S(1)} %get-tuple-element.56), channel_id=1, source_target_pairs={{0,32},{16,48},{32,0},{48,16},{64,96},{80,112},{96,64},{112,80},{1... | collective-permute-start | bytes 786440 | tf_op jit(solution)/shard_map/cond/branch_1_fun/ppermute | solution.py:27

commit v2 on v0

v2 whole, which is shorter than its diff:
```python
from functools import partial

import jax
import jax.numpy as jnp
from jax import lax
from jax.experimental import pallas as pl
from jax.experimental.pallas import tpu as pltpu
from jax.sharding import PartitionSpec as P

D = 4096
KW = 512
BITS = 3
CORES = 2
SPAN = 2
RINGS = 4
SIDES = CORES * SPAN
ROWS = D // (SIDES * RINGS)
HALF = D // CORES
SCALE = D ** (-0.5)
ALONG_Y = [[side + SIDES * y for y in range(RINGS)] for side in range(SIDES)]
IN_VMEM = pl.BlockSpec(memory_space=pltpu.VMEM)
IN_SMEM = pl.BlockSpec(memory_space=pltpu.SMEM)
PARAMS = pltpu.CompilerParams(vmem_limit_bytes=16 << 20)
LIGHT = pl.CostEstimate(flops=1 << 20, bytes_accessed=1 << 20, transcendentals=0)
HEAVY = pl.CostEstimate(flops=1 << 38, bytes_accessed=1 << 20, transcendentals=0)


def shaped(*shape, dtype=jnp.bfloat16):
    return jax.ShapeDtypeStruct(shape, dtype)


def local(kernel, outs, cost, scalars, *operands, scratch=()):
    return pl.pallas_call(
        kernel,
        in_specs=[IN_SMEM] + [IN_VMEM] * len(operands),
        out_specs=[IN_VMEM] * len(outs),
        out_shape=list(outs),
        scratch_shapes=list(scratch),
        compiler_params=PARAMS,
        cost_estimate=cost,
        name=kernel.__name__,
    )(scalars, *operands)


def swapped(block, axis, apart):
    count = lax.axis_size(axis)
    return lax.ppermute(block, axis, [(low, low ^ apart) for low in range(count)])


def along_y(block):
    return lax.all_to_all(block, "fsdp", 0, 0, tiled=True, axis_index_groups=ALONG_Y)


def shifted(block, hops):
    count = SIDES * RINGS
    return lax.ppermute(block, "fsdp", [(place, (place + SIDES * hops) % count) for place in range(count)])


def after(value, earlier):
    return lax.optimization_barrier((value, earlier))[0]


def columns(block):
    return pl.ds(pl.multiple_of(block * ROWS, ROWS), ROWS)


def pack(spot, inputs, cotan, packed):
    for k in range(SPAN * RINGS):
        packed[:, k * ROWS : (k + 1) * ROWS] = inputs[:, columns(CORES * k + 1 - spot[0])]
    packed[:, HALF:] = cotan[...]


def gradient_terms(spot, inputs, cotan, partner, own, kept, far, last):
    turned = cotan[...].T
    partner_turned = partner[:, HALF:].T
    for side, outs in ((1 - spot[1], (last, far, far, last)), (spot[1], (own, kept, kept, kept))):
        for hops in (2, 1, 3, 0):
            k = SPAN * lax.rem(spot[2] + hops, RINGS) + side
            total = jnp.dot(turned, inputs[:, columns(CORES * k + spot[0])], preferred_element_type=jnp.float32)
            total += jnp.dot(partner_turned, partner[:, columns(k)], preferred_element_type=jnp.float32)
            if outs[hops] is own:
                own[...] = total * SCALE
            elif outs[hops] is last:
                last[0 if hops else 1] = (total * SCALE).astype(jnp.bfloat16)
            else:
                outs[hops][hops - 1] = (total * SCALE).astype(jnp.bfloat16)


def fold_far(_, kept, far, first, second):
    for at, out in enumerate((first, second)):
        out[...] = (kept[at].astype(jnp.float32) + far[at].astype(jnp.float32)).astype(jnp.bfloat16)


def fold_last(_, kept, last, third):
    third[...] = (kept[2].astype(jnp.float32) + last[0].astype(jnp.float32)).astype(jnp.bfloat16)


def fold_own(_, own, last, home):
    home[...] = own[...] + last[1].astype(jnp.float32)


def update(rate, master, home, first, second, third, updated, short):
    near = home[...] + first[...].astype(jnp.float32)
    grad = near + (second[...].astype(jnp.float32) + third[...].astype(jnp.float32))
    new = master[...] - rate[0] * grad.T
    updated[...] = new
    short[...] = new.astype(jnp.bfloat16)


def mix(_, updated, other, mixed):
    mixed[...] = 0.5 * (updated[...] + other[...].astype(jnp.float32))


def own_copies(_, master, half, out):
    half[...] = master[...].astype(jnp.bfloat16)
    for y in range(RINGS):
        out[y] = half[...]


def near_copies(_, near, out):
    for y in range(RINGS):
        out[y] = near[...]


def keys(spot, inputs, cotan, mine, mine_near, theirs, theirs_near, forward, backward, total):
    core, across = spot[0], spot[1]
    over_width = (((1,), (1,)), ((), ()))
    sources = ((mine, across, core), (mine_near, 1 - across, core))
    sources += ((theirs, across, 1 - core), (theirs_near, 1 - across, 1 - core))
    total[...] = jnp.zeros_like(total)
    for y in range(RINGS):
        for rows, side, whose in sources:
            at = columns(SIDES * y + CORES * side + whose)
            total[...] += jnp.dot(inputs[:, at], rows[y], preferred_element_type=jnp.float32)
            back = lax.dot_general(cotan[...], rows[y], over_width, preferred_element_type=jnp.float32)
            backward[:, at] = (back * SCALE).astype(jnp.bfloat16)
    forward[...] = (total[...] * SCALE).astype(jnp.bfloat16)


def step(bit, inputs, master, cotan, rate):
    place = lax.axis_index("fsdp")
    spot = jnp.stack((place % CORES, place // CORES % SPAN, place // SIDES)).astype(jnp.int32)
    tokens = inputs.shape[0]
    block, wide = shaped(KW, ROWS), shaped(KW, ROWS, dtype=jnp.float32)
    copies = shaped(RINGS, ROWS, KW)

    (packed,) = local(pack, [shaped(tokens, HALF + KW)], LIGHT, spot, inputs, cotan)
    partner = swapped(packed, "fsdp", 1)
    half_weights, copied = local(own_copies, [shaped(ROWS, KW), copies], LIGHT, spot, master)
    near_weights = swapped(half_weights, "fsdp", CORES)
    mine = along_y(copied)

    own, kept, far, last = local(
        gradient_terms,
        [wide, shaped(3, KW, ROWS), shaped(2, KW, ROWS), shaped(2, KW, ROWS)],
        LIGHT, spot, inputs, cotan, partner,
    )
    far = swapped(far, "fsdp", CORES)
    (copied,) = local(near_copies, [copies], pl.CostEstimate(flops=1 << 32, bytes_accessed=1 << 20, transcendentals=0), spot, after(near_weights, own))
    mine_near = along_y(copied)
    last = swapped(after(last, copied), "fsdp", CORES)
    theirs = swapped(after(mine, own), "fsdp", 1)

    first, second = local(fold_far, [block] * 2, HEAVY, spot, kept, far)
    (third,) = local(fold_last, [block], HEAVY, spot, kept, after(last, first))
    (home,) = local(fold_own, [wide], HEAVY, spot, own, after(last, third))
    theirs_near = swapped(after(mine_near, third), "fsdp", 1)
    arrived = [shifted(part, hops) for hops, part in enumerate((first, second, third), 1)]
    updated, short = local(
        update, [shaped(ROWS, KW, dtype=jnp.float32), shaped(ROWS, KW)], LIGHT, rate[None], master, home, *arrived
    )
    other = swapped(short, "rep", 1 << bit)
    projected, input_grad = local(
        keys,
        [shaped(tokens, KW), shaped(tokens, D)],
        LIGHT, spot, inputs, cotan, mine, mine_near, theirs, theirs_near,
        scratch=[pltpu.VMEM((tokens, KW), jnp.float32)],
    )
    (mixed,) = local(mix, [shaped(ROWS, KW, dtype=jnp.float32)], LIGHT, spot, updated, after(other, projected))
    return (projected[None], input_grad[None], mixed[None])


def body(activations, weights, cotangent, step_index):
    rate = 0.3 / jnp.sqrt(1.0 + step_index[0].astype(jnp.float32) / 50.0)
    branches = [partial(step, bit) for bit in range(BITS)]
    return lax.switch(step_index[0] % BITS, branches, activations[0], weights[0], cotangent[0], rate)


def solution(mesh):
    return jax.shard_map(
        body,
        mesh=mesh,
        in_specs=(P("rep", "fsdp", None), P("rep", "fsdp", None), P("rep", "fsdp", None), P()),
        out_specs=(P("rep", "fsdp", None), P("rep", "fsdp", None), P("rep", "fsdp", None)),
        check_vma=False,
    )
```

time: 210 us -> 83.2 us (0.40)
  waiting for transfers between devices: 177 us -> 13.6 us
  starting transfers between devices: 2.29 us -> 46.4 us
  Pallas kernels: 0 us -> 20.7 us
  between operations: 14.8 us -> 1.3 us
  matrix products: 10.8 us -> 0 us
  other arithmetic: 2.72 us -> 0.08 us
  local copies, waits for them, and re-layouts: 2.34 us -> 0.03 us
    reduce_scatter x1 -> x0, waiting for transfers between devices: 105 us -> none  [body(): lax.psum_scatter((product * scale).astype(jnp.bfloat16), 'fsdp', scatter_...]
    all_gather x1 -> x0, waiting for transfers between devices: 66.2 us -> none  [body(): lax.all_gather(half_weights, 'fsdp', axis=0, tiled=True)]
    ppermute x1 -> x10, starting transfers between devices: 2.21 us -> 38 us  [the longest x7 26.5 us: swapped(): lax.ppermute(block, axis, [(low, low ^ apart) for low in range(count)])]
    pallas_call x0 -> x10, Pallas kernels: none -> 20.7 us  [local(): pl.pallas_call(kernel, in_specs=[IN_SMEM] + [IN_VMEM] * len(operands), ou...]
    dot_general x3 -> x0, matrix products: 10.8 us -> none  [the longest x1 4.19 us: body(): lax.dot_general(columns, cotan, (((0,), (0,)), ((), ())), preferred_eleme...]
    all_to_all x0 -> x2, starting transfers between devices: none -> 8.49 us  [along_y(): lax.all_to_all(block, 'fsdp', 0, 0, tiled=True, axis_index_groups=ALONG_Y)]
    all_to_all x0 -> x2, waiting for transfers between devices: none -> 5.11 us  [along_y(): lax.all_to_all(block, 'fsdp', 0, 0, tiled=True, axis_index_groups=ALONG_Y)]
    ppermute x1 -> x10, waiting for transfers between devices: 5.36 us -> 8.5 us  [the longest x7 8.49 us: swapped(): lax.ppermute(block, axis, [(low, low ^ apart) for low in range(count)])]
  transfers between devices with their start and end apart: 3 -> 12, of which waited for: 3 -> 3; matrix products, arithmetic and copies ran while one was open for 1% -> 0% of each run, Pallas kernels for 0% -> 21%
where the time goes in v2:
time: 83.2 us; the launch traced here: 82.5 us
  starting transfers between devices  46.4 us (56%)
  Pallas kernels  20.7 us (25%)
  waiting for transfers between devices  13.6 us (16%)
  between operations  1.3 us (2%)
    ppermute x7, starting transfers between devices, swapped(): lax.ppermute(block, axis, [(low, low ^ apart) for low in range(count)])  26.5 us
    pallas_call x10, Pallas kernels, local(): pl.pallas_call(kernel, in_specs=[IN_SMEM] + [IN_VMEM] * len(operands), ou...  20.7 us
    ppermute x3, starting transfers between devices, shifted(): lax.ppermute(block, 'fsdp', [(place, (place + SIDES * hops) % count) for...  11.5 us
    ppermute x7, waiting for transfers between devices, swapped(): lax.ppermute(block, axis, [(low, low ^ apart) for low in range(count)])  8.49 us
    all_to_all x2, starting transfers between devices, along_y(): lax.all_to_all(block, 'fsdp', 0, 0, tiled=True, axis_index_groups=ALONG_Y)  8.49 us
    all_to_all x2, waiting for transfers between devices, along_y(): lax.all_to_all(block, 'fsdp', 0, 0, tiled=True, axis_index_groups=ALONG_Y)  5.11 us
  transfers between devices with their start and end apart: 12, of which 3 were waited for; matrix products, arithmetic and copies ran while one was open for 0% of the time, Pallas kernels for 21%

profile of v2, /device:TPU:1, one launch (start us, length us, event | category | flops | bytes accessed | tf_op | source)
XLA Modules:
  0.0 82.5 jit_solution(990405982231451288)
XLA Ops:
  1.3 81.2 %conditional.1 = (bf16[1,192,512]{2,1,0:T(8,128)(2,1)}, bf16[1,192,4096]{2,1,0:T(8,128)(2,1)}, f32[1,256,512]{2,1,0:T(8,128)}) conditional(s32[]{:T(128)} %clamp.3, (f32[1,256,512]{2,1,0:T(8,128)}, bf16[1,192,4096]{2,1,0:T(8,128)(2,1)}, bf16[1,192,512]{2,1,0:T(8,128)(2,1)}, (), f32[1]{0:T(128)}, /*index=5*/(), ()) %tuple.40, ...), branch_computations={%region_0.1_spmd, %region_1.2_spmd, %region_2.3_spmd} | conditional | flops 828934979584 | bytes 49808448 | solution.py:186
  1.5 1.6 %pack.5 = bf16[192,2560]{1,0:T(8,128)(2,1)S(1)} custom-call(s32[3]{0:T(128)S(1)} %pad_add_fusion.2._.spot, bf16[192,4096]{1,0:T(8,128)(2,1)} %bitcast.34, bf16[192,512]{1,0:T(8,128)(2,1)} %bitcast.49), custom_call_target="tpu_custom_call" | custom-call | flops 1048576 | bytes 1048576 | tf_op jit(solution)/shard_map/cond/branch_2_fun/pack/pallas_call | solution.py:33
  3.0 8.8 %collective-permute-start.21 = (bf16[192,2560]{1,0:T(8,128)(2,1)S(1)}, bf16[192,2560]{1,0:T(8,128)(2,1)S(1)}, u32[]{:S(2)}, u32[]{:S(2)}) collective-permute-start(bf16[192,2560]{1,0:T(8,128)(2,1)S(1)} %pack.5), channel_id=1, source_target_pairs={{0,1},{1,0},{2,3},{3,2},{4,5},{5,4},{6,7},{7,6},{8,9},{9,8},{10,11... | collective-permute-start | bytes 2949128 | tf_op jit(solution)/shard_map/cond/branch_2_fun/ppermute | solution.py:47
  11.8 1.6 %own_copies.5 = (bf16[256,512]{1,0:T(8,128)(2,1)S(1)}, bf16[4,256,512]{2,1,0:T(8,128)(2,1)}) custom-call(s32[3]{0:T(128)S(1)} %pad_add_fusion.2._.spot, f32[256,512]{1,0:T(8,128)S(1)} %bitcast.41), custom_call_target="tpu_custom_call" | custom-call | flops 1048576 | bytes 1048576 | tf_op jit(solution)/shard_map/cond/branch_2_fun/own_copies/pallas_call | solution.py:33
  13.4 4.2 %all-to-all-start.4 = ((bf16[4,256,512]{2,1,0:T(8,128)(2,1)}), bf16[4,256,512]{2,1,0:T(8,128)(2,1)}, u32[]{:S(2)}, u32[]{:S(2)}) async-start(bf16[4,256,512]{2,1,0:T(8,128)(2,1)} %get-tuple-element.73), calls=%async_computation.4 | async-start | bytes 2097152 | tf_op jit(solution)/shard_map/cond/branch_2_fun/all_to_all | solution.py:51
  17.7 2.1 %collective-permute-start.20 = (bf16[256,512]{1,0:T(8,128)(2,1)S(1)}, bf16[256,512]{1,0:T(8,128)(2,1)S(1)}, u32[]{:S(2)}, u32[]{:S(2)}) collective-permute-start(bf16[256,512]{1,0:T(8,128)(2,1)S(1)} %get-tuple-element.74), channel_id=1, source_target_pairs={{0,2},{1,3},{2,0},{3,1},{4,6},{5,7},{6,4},{7,5},{8,10},{9,11},{10,... | collective-permute-start | bytes 786440 | tf_op jit(solution)/shard_map/cond/branch_2_fun/ppermute | solution.py:47
  19.8 3.2 %gradient_terms.5 = (f32[512,256]{1,0:T(8,128)S(1)}, bf16[3,512,256]{2,1,0:T(8,128)(2,1)S(1)}, bf16[2,512,256]{2,1,0:T(8,128)(2,1)S(1)}, bf16[2,512,256]{2,1,0:T(8,128)(2,1)}) custom-call(s32[3]{0:T(128)S(1)} %pad_add_fusion.2._.spot, bf16[192,4096]{1,0:T(8,128)(2,1)} %bitcast.35, bf16[192,512]{1,0:T(8,128)(2,1)} %bitcast.50, ...), custom_call_target="tpu_custom_call" | custom-call | flops 1048576 | bytes 1048576 | tf_op jit(solution)/shard_map/cond/branch_2_fun/gradient_terms/pallas_call | solution.py:33
  23.0 4.8 %collective-permute-start.24 = (bf16[2,512,256]{2,1,0:T(8,128)(2,1)S(1)}, bf16[2,512,256]{2,1,0:T(8,128)(2,1)S(1)}, u32[]{:S(2)}, u32[]{:S(2)}) collective-permute-start(bf16[2,512,256]{2,1,0:T(8,128)(2,1)S(1)} %get-tuple-element.81), channel_id=1, source_target_pairs={{0,2},{1,3},{2,0},{3,1},{4,6},{5,7},{6,4},{7,5},{8,10},{9,11},{10,... | collective-permute-start | bytes 1572872 | tf_op jit(solution)/shard_map/cond/branch_2_fun/ppermute | solution.py:47
  27.9 5.1 %all-to-all-done.4.mine = bf16[4,256,512]{2,1,0:T(8,128)(2,1)} async-done(((bf16[4,256,512]{2,1,0:T(8,128)(2,1)}), bf16[4,256,512]{2,1,0:T(8,128)(2,1)}, u32[]{:S(2)}, u32[]{:S(2)}) %all-to-all-start.4) | async-done | bytes 1048608 | tf_op jit(solution)/shard_map/cond/branch_2_fun/all_to_all | solution.py:51
  33.0 1.6 %near_copies.5 = bf16[4,256,512]{2,1,0:T(8,128)(2,1)} custom-call(s32[3]{0:T(128)S(1)} %pad_add_fusion.2._.spot, bf16[256,512]{1,0:T(8,128)(2,1)S(1)} %collective-permute-done.20.near), custom_call_target="tpu_custom_call" | custom-call | flops 4294967296 | bytes 1048576 | tf_op jit(solution)/shard_map/cond/branch_2_fun/near_copies/pallas_call | solution.py:33
  34.6 4.3 %all-to-all-start.5 = ((bf16[4,256,512]{2,1,0:T(8,128)(2,1)}), bf16[4,256,512]{2,1,0:T(8,128)(2,1)}, u32[]{:S(2)}, u32[]{:S(2)}) async-start(bf16[4,256,512]{2,1,0:T(8,128)(2,1)} %near_copies.5), calls=%async_computation.5 | async-start | bytes 2097152 | tf_op jit(solution)/shard_map/cond/branch_2_fun/all_to_all | solution.py:51
  38.8 1.9 %collective-permute-start.23 = (bf16[2,512,256]{2,1,0:T(8,128)(2,1)}, bf16[2,512,256]{2,1,0:T(8,128)(2,1)}, u32[]{:S(2)}, u32[]{:S(2)}) collective-permute-start(bf16[2,512,256]{2,1,0:T(8,128)(2,1)} %get-tuple-element.80), channel_id=1, source_target_pairs={{0,2},{1,3},{2,0},{3,1},{4,6},{5,7},{6,4},{7,5},{8,10},{9,11},{10,... | collective-permute-start | bytes 1572872 | tf_op jit(solution)/shard_map/cond/branch_2_fun/ppermute | solution.py:47
  40.8 2.7 %collective-permute-start.22 = (bf16[4,256,512]{2,1,0:T(8,128)(2,1)}, bf16[4,256,512]{2,1,0:T(8,128)(2,1)}, u32[]{:S(2)}, u32[]{:S(2)}) collective-permute-start(bf16[4,256,512]{2,1,0:T(8,128)(2,1)} %all-to-all-done.4.mine), channel_id=1, source_target_pairs={{0,1},{1,0},{2,3},{3,2},{4,5},{5,4},{6,7},{7,6},{8,9},{9,8},{10,11... | collective-permute-start | bytes 3145736 | tf_op jit(solution)/shard_map/cond/branch_2_fun/ppermute | solution.py:47
  43.5 1.4 %fold_far.5 = (bf16[512,256]{1,0:T(8,128)(2,1)}, bf16[512,256]{1,0:T(8,128)(2,1)}) custom-call(s32[3]{0:T(128)S(1)} %pad_add_fusion.2._.spot, bf16[3,512,256]{2,1,0:T(8,128)(2,1)S(1)} %get-tuple-element.78.kept, bf16[2,512,256]{2,1,0:T(8,128)(2,1)S(1)} %collective-permute-done.24.far), custom_call_target="tpu_custom_call" | custom-call | flops 274877906944 | bytes 1048576 | tf_op jit(solution)/shard_map/cond/branch_2_fun/fold_far/pallas_call | solution.py:33
  44.9 5.1 %collective-permute-start.27 = (bf16[512,256]{1,0:T(8,128)(2,1)}, bf16[512,256]{1,0:T(8,128)(2,1)}, u32[]{:S(2)}, u32[]{:S(2)}) collective-permute-start(bf16[512,256]{1,0:T(8,128)(2,1)} %get-tuple-element.89), channel_id=1, source_target_pairs={{0,8},{1,9},{2,10},{3,11},{4,12},{5,13},{6,14},{7,15},{8,0},{9,1},... | collective-permute-start | bytes 786440 | tf_op jit(solution)/shard_map/cond/branch_2_fun/ppermute | solution.py:56
  50.0 2.2 %collective-permute-start.26 = (bf16[512,256]{1,0:T(8,128)(2,1)}, bf16[512,256]{1,0:T(8,128)(2,1)}, u32[]{:S(2)}, u32[]{:S(2)}) collective-permute-start(bf16[512,256]{1,0:T(8,128)(2,1)} %get-tuple-element.82), channel_id=1, source_target_pairs={{0,4},{1,5},{2,6},{3,7},{4,8},{5,9},{6,10},{7,11},{8,12},{9,13},{1... | collective-permute-start | bytes 786440 | tf_op jit(solution)/shard_map/cond/branch_2_fun/ppermute | solution.py:56
  52.2 3.0 %collective-permute-done.23.last = bf16[2,512,256]{2,1,0:T(8,128)(2,1)} collective-permute-done((bf16[2,512,256]{2,1,0:T(8,128)(2,1)}, bf16[2,512,256]{2,1,0:T(8,128)(2,1)}, u32[]{:S(2)}, u32[]{:S(2)}) %collective-permute-start.23) | collective-permute-done | bytes 524320 | tf_op jit(solution)/shard_map/cond/branch_2_fun/ppermute | solution.py:47
  55.2 1.8 %fold_last.5 = bf16[512,256]{1,0:T(8,128)(2,1)} custom-call(s32[3]{0:T(128)S(1)} %pad_add_fusion.2._.spot, bf16[3,512,256]{2,1,0:T(8,128)(2,1)S(1)} %get-tuple-element.78.kept, bf16[2,512,256]{2,1,0:T(8,128)(2,1)} %collective-permute-done.23.last), custom_call_target="tpu_custom_call" | custom-call | flops 274877906944 | bytes 1048576 | tf_op jit(solution)/shard_map/cond/branch_2_fun/fold_last/pallas_call | solution.py:33
  57.0 4.2 %collective-permute-start.28 = (bf16[512,256]{1,0:T(8,128)(2,1)}, bf16[512,256]{1,0:T(8,128)(2,1)}, u32[]{:S(2)}, u32[]{:S(2)}) collective-permute-start(bf16[512,256]{1,0:T(8,128)(2,1)} %fold_last.5), channel_id=1, source_target_pairs={{0,12},{1,13},{2,14},{3,15},{4,0},{5,1},{6,2},{7,3},{8,4},{9,5},{1... | collective-permute-start | bytes 786440 | tf_op jit(solution)/shard_map/cond/branch_2_fun/ppermute | solution.py:56
  61.2 4.2 %collective-permute-start.25 = (bf16[4,256,512]{2,1,0:T(8,128)(2,1)}, bf16[4,256,512]{2,1,0:T(8,128)(2,1)}, u32[]{:S(2)}, u32[]{:S(2)}) collective-permute-start(bf16[4,256,512]{2,1,0:T(8,128)(2,1)} %all-to-all-done.5.mine_near), channel_id=1, source_target_pairs={{0,1},{1,0},{2,3},{3,2},{4,5},{5,4},{6,7},{7,6},{8,9},{9,8},{10,11... | collective-permute-start | bytes 3145736 | tf_op jit(solution)/shard_map/cond/branch_2_fun/ppermute | solution.py:47
  66.7 1.5 %update.5 = (f32[256,512]{1,0:T(8,128)S(1)}, bf16[256,512]{1,0:T(8,128)(2,1)S(1)}) custom-call(f32[1]{0:T(128)S(6)} %div.59.rate, f32[256,512]{1,0:T(8,128)S(1)} %bitcast.42, f32[512,256]{1,0:T(8,128)S(1)} %fold_own.5.home, bf16[512,256]{1,0:T(8,128)(2,1)} %collective-permute-done.26.first, bf16[512,256]{1,0:T(8,128)(2,1)} %collective-permute-done.27.second, ...), custom_call_target="tpu_custom_call" | custom-call | flops 1048576 | bytes 1048576 | tf_op jit(solution)/shard_map/cond/branch_2_fun/update/pallas_call | solution.py:33
  68.2 1.9 %collective-permute-start.29 = (bf16[256,512]{1,0:T(8,128)(2,1)S(1)}, bf16[256,512]{1,0:T(8,128)(2,1)S(1)}, u32[]{:S(2)}, u32[]{:S(2)}) collective-permute-start(bf16[256,512]{1,0:T(8,128)(2,1)S(1)} %get-tuple-element.91), channel_id=1, source_target_pairs={{0,64},{16,80},{32,96},{48,112},{64,0},{80,16},{96,32},{112,48},{1... | collective-permute-start | bytes 786440 | tf_op jit(solution)/shard_map/cond/branch_2_fun/ppermute | solution.py:47
  70.1 5.5 %keys.5 = (bf16[192,512]{1,0:T(8,128)(2,1)}, bf16[192,4096]{1,0:T(8,128)(2,1)}) custom-call(s32[3]{0:T(128)S(1)} %pad_add_fusion.2._.spot, bf16[192,4096]{1,0:T(8,128)(2,1)S(1)} %bitcast.36, bf16[192,512]{1,0:T(8,128)(2,1)S(1)} %bitcast.51, bf16[4,256,512]{2,1,0:T(8,128)(2,1)} %all-to-all-done.4.mine, bf16[4,256,512]{2,1,0:T(8,128)(2,1)} %all-to-all-done.5.mine_near, ...), custom_call_target="tpu_custom_call" | custom-call | flops 1048576 | bytes 1048576 | tf_op jit(solution)/shard_map/cond/branch_2_fun/keys/pallas_call | solution.py:33
  75.7 5.4 %collective-permute-done.29.other = bf16[256,512]{1,0:T(8,128)(2,1)S(1)} collective-permute-done((bf16[256,512]{1,0:T(8,128)(2,1)S(1)}, bf16[256,512]{1,0:T(8,128)(2,1)S(1)}, u32[]{:S(2)}, u32[]{:S(2)}) %collective-permute-start.29) | collective-permute-done | bytes 262176 | tf_op jit(solution)/shard_map/cond/branch_2_fun/ppermute | solution.py:47
  (20 shorter events, 2.7 us)
Async XLA Ops:
  1.3 10.5 %copy-start.7 = (f32[1,256,512]{2,1,0:T(8,128)S(1)}, f32[1,256,512]{2,1,0:T(8,128)}, u32[]{:S(2)}) copy-start(f32[1,256,512]{2,1,0:T(8,128)} %get-tuple-element.128) | copy-start | bytes 1572868 | tf_op jit(solution)/shard_map/cond
  3.0 16.8 %collective-permute-start.21 = (bf16[192,2560]{1,0:T(8,128)(2,1)S(1)}, bf16[192,2560]{1,0:T(8,128)(2,1)S(1)}, u32[]{:S(2)}, u32[]{:S(2)}) collective-permute-start(bf16[192,2560]{1,0:T(8,128)(2,1)S(1)} %pack.5), channel_id=1, source_target_pairs={{0,1},{1,0},{2,3},{3,2},{4,5},{5,4},{6,7},{7,6},{8,9},{9,8},{10,11... | collective-permute-start | bytes 2949128 | tf_op jit(solution)/shard_map/cond/branch_2_fun/ppermute | solution.py:47
  13.4 19.6 %all-to-all-start.4 = ((bf16[4,256,512]{2,1,0:T(8,128)(2,1)}), bf16[4,256,512]{2,1,0:T(8,128)(2,1)}, u32[]{:S(2)}, u32[]{:S(2)}) async-start(bf16[4,256,512]{2,1,0:T(8,128)(2,1)} %get-tuple-element.73), calls=%async_computation.4 | async-start | bytes 2097152 | tf_op jit(solution)/shard_map/cond/branch_2_fun/all_to_all | solution.py:51
  17.7 15.3 %collective-permute-start.20 = (bf16[256,512]{1,0:T(8,128)(2,1)S(1)}, bf16[256,512]{1,0:T(8,128)(2,1)S(1)}, u32[]{:S(2)}, u32[]{:S(2)}) collective-permute-start(bf16[256,512]{1,0:T(8,128)(2,1)S(1)} %get-tuple-element.74), channel_id=1, source_target_pairs={{0,2},{1,3},{2,0},{3,1},{4,6},{5,7},{6,4},{7,5},{8,10},{9,11},{10,... | collective-permute-start | bytes 786440 | tf_op jit(solution)/shard_map/cond/branch_2_fun/ppermute | solution.py:47
  23.0 20.5 %collective-permute-start.24 = (bf16[2,512,256]{2,1,0:T(8,128)(2,1)S(1)}, bf16[2,512,256]{2,1,0:T(8,128)(2,1)S(1)}, u32[]{:S(2)}, u32[]{:S(2)}) collective-permute-start(bf16[2,512,256]{2,1,0:T(8,128)(2,1)S(1)} %get-tuple-element.81), channel_id=1, source_target_pairs={{0,2},{1,3},{2,0},{3,1},{4,6},{5,7},{6,4},{7,5},{8,10},{9,11},{10,... | collective-permute-start | bytes 1572872 | tf_op jit(solution)/shard_map/cond/branch_2_fun/ppermute | solution.py:47
  34.6 26.7 %all-to-all-start.5 = ((bf16[4,256,512]{2,1,0:T(8,128)(2,1)}), bf16[4,256,512]{2,1,0:T(8,128)(2,1)}, u32[]{:S(2)}, u32[]{:S(2)}) async-start(bf16[4,256,512]{2,1,0:T(8,128)(2,1)} %near_copies.5), calls=%async_computation.5 | async-start | bytes 2097152 | tf_op jit(solution)/shard_map/cond/branch_2_fun/all_to_all | solution.py:51
  38.8 16.4 %collective-permute-start.23 = (bf16[2,512,256]{2,1,0:T(8,128)(2,1)}, bf16[2,512,256]{2,1,0:T(8,128)(2,1)}, u32[]{:S(2)}, u32[]{:S(2)}) collective-permute-start(bf16[2,512,256]{2,1,0:T(8,128)(2,1)} %get-tuple-element.80), channel_id=1, source_target_pairs={{0,2},{1,3},{2,0},{3,1},{4,6},{5,7},{6,4},{7,5},{8,10},{9,11},{10,... | collective-permute-start | bytes 1572872 | tf_op jit(solution)/shard_map/cond/branch_2_fun/ppermute | solution.py:47
  40.8 29.3 %collective-permute-start.22 = (bf16[4,256,512]{2,1,0:T(8,128)(2,1)}, bf16[4,256,512]{2,1,0:T(8,128)(2,1)}, u32[]{:S(2)}, u32[]{:S(2)}) collective-permute-start(bf16[4,256,512]{2,1,0:T(8,128)(2,1)} %all-to-all-done.4.mine), channel_id=1, source_target_pairs={{0,1},{1,0},{2,3},{3,2},{4,5},{5,4},{6,7},{7,6},{8,9},{9,8},{10,11... | collective-permute-start | bytes 3145736 | tf_op jit(solution)/shard_map/cond/branch_2_fun/ppermute | solution.py:47
  44.9 21.8 %collective-permute-start.27 = (bf16[512,256]{1,0:T(8,128)(2,1)}, bf16[512,256]{1,0:T(8,128)(2,1)}, u32[]{:S(2)}, u32[]{:S(2)}) collective-permute-start(bf16[512,256]{1,0:T(8,128)(2,1)} %get-tuple-element.89), channel_id=1, source_target_pairs={{0,8},{1,9},{2,10},{3,11},{4,12},{5,13},{6,14},{7,15},{8,0},{9,1},... | collective-permute-start | bytes 786440 | tf_op jit(solution)/shard_map/cond/branch_2_fun/ppermute | solution.py:56
  50.0 16.7 %collective-permute-start.26 = (bf16[512,256]{1,0:T(8,128)(2,1)}, bf16[512,256]{1,0:T(8,128)(2,1)}, u32[]{:S(2)}, u32[]{:S(2)}) collective-permute-start(bf16[512,256]{1,0:T(8,128)(2,1)} %get-tuple-element.82), channel_id=1, source_target_pairs={{0,4},{1,5},{2,6},{3,7},{4,8},{5,9},{6,10},{7,11},{8,12},{9,13},{1... | collective-permute-start | bytes 786440 | tf_op jit(solution)/shard_map/cond/branch_2_fun/ppermute | solution.py:56
  57.0 9.6 %collective-permute-start.28 = (bf16[512,256]{1,0:T(8,128)(2,1)}, bf16[512,256]{1,0:T(8,128)(2,1)}, u32[]{:S(2)}, u32[]{:S(2)}) collective-permute-start(bf16[512,256]{1,0:T(8,128)(2,1)} %fold_last.5), channel_id=1, source_target_pairs={{0,12},{1,13},{2,14},{3,15},{4,0},{5,1},{6,2},{7,3},{8,4},{9,5},{1... | collective-permute-start | bytes 786440 | tf_op jit(solution)/shard_map/cond/branch_2_fun/ppermute | solution.py:56
  61.2 8.9 %collective-permute-start.25 = (bf16[4,256,512]{2,1,0:T(8,128)(2,1)}, bf16[4,256,512]{2,1,0:T(8,128)(2,1)}, u32[]{:S(2)}, u32[]{:S(2)}) collective-permute-start(bf16[4,256,512]{2,1,0:T(8,128)(2,1)} %all-to-all-done.5.mine_near), channel_id=1, source_target_pairs={{0,1},{1,0},{2,3},{3,2},{4,5},{5,4},{6,7},{7,6},{8,9},{9,8},{10,11... | collective-permute-start | bytes 3145736 | tf_op jit(solution)/shard_map/cond/branch_2_fun/ppermute | solution.py:47
  65.4 1.2 %copy-start.8 = (f32[1,256,512]{2,1,0:T(8,128)S(1)}, f32[1,256,512]{2,1,0:T(8,128)}, u32[]{:S(2)}) copy-start(f32[1,256,512]{2,1,0:T(8,128)} %get-tuple-element.128) | copy-start | bytes 1572868 | tf_op jit(solution)/shard_map/cond
  66.6 3.5 %copy-start.2 = (bf16[1,192,4096]{2,1,0:T(8,128)(2,1)S(1)}, bf16[1,192,4096]{2,1,0:T(8,128)(2,1)}, u32[]{:S(2)}) copy-start(bf16[1,192,4096]{2,1,0:T(8,128)(2,1)} %get-tuple-element.131) | copy-start | bytes 4718596 | tf_op jit(solution)/shard_map/cond
  66.6 3.5 %copy-start.11 = (bf16[1,192,512]{2,1,0:T(8,128)(2,1)S(1)}, bf16[1,192,512]{2,1,0:T(8,128)(2,1)}, u32[]{:S(2)}) copy-start(bf16[1,192,512]{2,1,0:T(8,128)(2,1)} %get-tuple-element.134) | copy-start | bytes 589828 | tf_op jit(solution)/shard_map/cond
  68.2 13.0 %collective-permute-start.29 = (bf16[256,512]{1,0:T(8,128)(2,1)S(1)}, bf16[256,512]{1,0:T(8,128)(2,1)S(1)}, u32[]{:S(2)}, u32[]{:S(2)}) collective-permute-start(bf16[256,512]{1,0:T(8,128)(2,1)S(1)} %get-tuple-element.91), channel_id=1, source_target_pairs={{0,64},{16,80},{32,96},{48,112},{64,0},{80,16},{96,32},{112,48},{1... | collective-permute-start | bytes 786440 | tf_op jit(solution)/shard_map/cond/branch_2_fun/ppermute | solution.py:47

commit v3 on v2

v3 whole, which is shorter than its diff:
```python
from functools import partial

import jax
import jax.numpy as jnp
from jax import lax
from jax.experimental import pallas as pl
from jax.experimental.pallas import tpu as pltpu
from jax.sharding import PartitionSpec as P

D = 4096
KW = 512
BITS = 3
CORES = 2
SPAN = 2
RINGS = 4
SIDES = CORES * SPAN
ROWS = D // (SIDES * RINGS)
HALF = D // CORES
SCALE = D ** (-0.5)
ALONG_Y = [[side + SIDES * y for y in range(RINGS)] for side in range(SIDES)]
IN_VMEM = pl.BlockSpec(memory_space=pltpu.VMEM)
IN_SMEM = pl.BlockSpec(memory_space=pltpu.SMEM)
PARAMS = pltpu.CompilerParams(vmem_limit_bytes=16 << 20)
LIGHT = pl.CostEstimate(flops=1 << 20, bytes_accessed=1 << 20, transcendentals=0)
HEAVY = pl.CostEstimate(flops=1 << 38, bytes_accessed=1 << 32, transcendentals=0)
MEDIUM = pl.CostEstimate(flops=1 << 33, bytes_accessed=1 << 26, transcendentals=0)
FOLD = pl.CostEstimate(flops=1 << 38, bytes_accessed=1 << 20, transcendentals=0)


def shaped(*shape, dtype=jnp.bfloat16):
    return jax.ShapeDtypeStruct(shape, dtype)


def close(*shape, dtype=jnp.bfloat16):
    return pltpu.VMEM(shape, dtype)


def held(block):
    return pltpu.with_memory_space_constraint(block, pltpu.VMEM)


def local(kernel, outs, cost, scalars, *operands, scratch=()):
    return pl.pallas_call(
        kernel,
        in_specs=[IN_SMEM] + [IN_VMEM] * len(operands),
        out_specs=[IN_VMEM] * len(outs),
        out_shape=list(outs),
        scratch_shapes=list(scratch),
        compiler_params=PARAMS,
        cost_estimate=cost,
        name=kernel.__name__,
    )(scalars, *operands)


def swapped(block, axis, apart):
    count = lax.axis_size(axis)
    return lax.ppermute(block, axis, [(low, low ^ apart) for low in range(count)])


def along_y(block):
    return lax.all_to_all(block, "fsdp", 0, 0, tiled=True, axis_index_groups=ALONG_Y)


def shifted(block, hops):
    count = SIDES * RINGS
    return lax.ppermute(block, "fsdp", [(place, (place + SIDES * hops) % count) for place in range(count)])


def after(value, earlier):
    return lax.optimization_barrier((value, earlier))[0]


def columns(block):
    return pl.ds(pl.multiple_of(block * ROWS, ROWS), ROWS)


def pack(spot, inputs, cotan, packed):
    for k in range(SPAN * RINGS):
        packed[:, k * ROWS : (k + 1) * ROWS] = inputs[:, columns(CORES * k + 1 - spot[0])]
    packed[:, HALF:] = cotan[...]


def gradient_terms(spot, inputs, cotan, partner, kept, given):
    turned = cotan[...].T
    partner_turned = partner[:, HALF:].T
    for out, side in ((given, 1 - spot[1]), (kept, spot[1])):
        for y in range(RINGS):
            k = SPAN * y + side
            total = jnp.dot(turned, inputs[:, columns(CORES * k + spot[0])], preferred_element_type=jnp.float32)
            total += jnp.dot(partner_turned, partner[:, columns(k)], preferred_element_type=jnp.float32)
            out[y] = (total * SCALE).astype(jnp.bfloat16)


def fold(_, kept, taken, both):
    for y in range(RINGS):
        both[y] = (kept[y].astype(jnp.float32) + taken[y].astype(jnp.float32)).astype(jnp.bfloat16)


def update(rate, master, terms, updated, short):
    parts = [terms[y].astype(jnp.float32) for y in range(RINGS)]
    grad = (parts[0] + parts[1]) + (parts[2] + parts[3])
    new = master[...] - rate[0] * grad.T
    updated[...] = new
    short[...] = new.astype(jnp.bfloat16)


def mix(_, updated, other, mixed):
    mixed[...] = 0.5 * (updated[...] + other[...].astype(jnp.float32))


def pair_up(_, half, near, pair):
    pair[0] = half[...]
    pair[1] = near[...]


def gather(_, *refs):
    for hops, piece in enumerate(refs[:-1]):
        refs[-1][hops] = piece[...]


def keys(spot, inputs, cotan, mine, theirs, forward, backward, total):
    over_width = (((1,), (1,)), ((), ()))
    total[...] = jnp.zeros_like(total)
    for hops in range(RINGS):
        y = lax.rem(spot[2] + RINGS - hops, RINGS)
        for side in range(SPAN):
            for rows, core in ((mine, spot[0]), (theirs, 1 - spot[0])):
                at = columns(SIDES * y + CORES * (spot[1] ^ side) + core)
                part = rows[hops, side]
                total[...] += jnp.dot(inputs[:, at], part, preferred_element_type=jnp.float32)
                back = lax.dot_general(cotan[...], part, over_width, preferred_element_type=jnp.float32)
                backward[:, at] = (back * SCALE).astype(jnp.bfloat16)
    forward[...] = (total[...] * SCALE).astype(jnp.bfloat16)


def step(bit, inputs, master, cotan, rate):
    place = lax.axis_index("fsdp")
    spot = jnp.stack((place % CORES, place // CORES % SPAN, place // SIDES)).astype(jnp.int32)
    tokens = inputs.shape[0]
    block, wide = close(KW, ROWS), close(KW, ROWS, dtype=jnp.float32)

    (packed,) = local(pack, [close(tokens, HALF + KW)], LIGHT, spot, inputs, cotan)
    partner = swapped(packed, "fsdp", 1)
    half_weights = master.astype(jnp.bfloat16)
    near_weights = swapped(half_weights, "fsdp", CORES)

    kept, given = local(
        gradient_terms, [close(RINGS, KW, ROWS)] * 2, LIGHT, spot, inputs, cotan, held(partner)
    )
    taken = swapped(given, "fsdp", CORES)
    (pair,) = local(pair_up, [close(SPAN, ROWS, KW)], MEDIUM, spot, half_weights, held(after(near_weights, kept)))
    pieces = [shifted(pair, hops) for hops in (1, 2, 3)]

    (both,) = local(fold, [close(RINGS, KW, ROWS)], FOLD, spot, kept, held(taken))
    terms = along_y(both)
    (mine,) = local(gather, [close(RINGS, SPAN, ROWS, KW)], MEDIUM, spot, pair, *map(held, [after(piece, both) for piece in pieces]))
    theirs = swapped(mine, "fsdp", 1)
    updated, short = local(
        update, [close(ROWS, KW, dtype=jnp.float32), close(ROWS, KW)], HEAVY, rate[None], master, held(terms)
    )
    other = swapped(short, "rep", 1 << bit)
    projected, input_grad = local(
        keys,
        [shaped(tokens, KW), shaped(tokens, D)],
        LIGHT, spot, inputs, cotan, held(mine), held(theirs),
        scratch=[pltpu.VMEM((tokens, KW), jnp.float32)],
    )
    (mixed,) = local(mix, [shaped(ROWS, KW, dtype=jnp.float32)], LIGHT, spot, updated, held(after(other, projected)))
    return (projected[None], input_grad[None], mixed[None])


def body(activations, weights, cotangent, step_index):
    rate = 0.3 / jnp.sqrt(1.0 + step_index[0].astype(jnp.float32) / 50.0)
    branches = [partial(step, bit) for bit in range(BITS)]
    return lax.switch(step_index[0] % BITS, branches, activations[0], weights[0], cotangent[0], rate)


def solution(mesh):
    return jax.shard_map(
        body,
        mesh=mesh,
        in_specs=(P("rep", "fsdp", None), P("rep", "fsdp", None), P("rep", "fsdp", None), P()),
        out_specs=(P("rep", "fsdp", None), P("rep", "fsdp", None), P("rep", "fsdp", None)),
        check_vma=False,
    )
```

time: 83.2 us -> 75.9 us (0.912)
  starting transfers between devices: 46.4 us -> 30.7 us
  waiting for transfers between devices: 13.6 us -> 26.3 us
  Pallas kernels: 20.7 us -> 16.8 us
    ppermute x7 -> x5, waiting for transfers between devices: 8.49 us -> 17.4 us  [swapped(): lax.ppermute(block, axis, [(low, low ^ apart) for low in range(count)])]
    ppermute x7 -> x5, starting transfers between devices: 26.5 us -> 19.9 us  [swapped(): lax.ppermute(block, axis, [(low, low ^ apart) for low in range(count)])]
    all_to_all x2 -> x1, starting transfers between devices: 8.49 us -> 3.52 us  [along_y(): lax.all_to_all(block, 'fsdp', 0, 0, tiled=True, axis_index_groups=ALONG_Y)]
    ppermute x3, starting transfers between devices: 11.5 us -> 7.2 us  [shifted(): lax.ppermute(block, 'fsdp', [(place, (place + SIDES * hops) % count) for...]
    ppermute x3, waiting for transfers between devices: 0.01 us -> 4.2 us  [shifted(): lax.ppermute(block, 'fsdp', [(place, (place + SIDES * hops) % count) for...]
    pallas_call x10 -> x8, Pallas kernels: 20.7 us -> 16.8 us  [local(): pl.pallas_call(kernel, in_specs=[IN_SMEM] + [IN_VMEM] * len(operands), ou...]
    all_to_all x2 -> x1, waiting for transfers between devices: 5.11 us -> 4.72 us  [along_y(): lax.all_to_all(block, 'fsdp', 0, 0, tiled=True, axis_index_groups=ALONG_Y)]
  transfers between devices with their start and end apart: 12 -> 9, of which waited for: 3 -> 6; matrix products, arithmetic and copies ran while one was open for 0% -> 0% of each run, Pallas kernels for 21% -> 18%
where the time goes in v3:
time: 75.9 us; the launch traced here: 75.5 us
  starting transfers between devices  30.7 us (40%)
  waiting for transfers between devices  26.3 us (35%)
  Pallas kernels  16.8 us (22%)
  between operations  1.3 us (2%)
    ppermute x5, starting transfers between devices, swapped(): lax.ppermute(block, axis, [(low, low ^ apart) for low in range(count)])  19.9 us
    ppermute x5, waiting for transfers between devices, swapped(): lax.ppermute(block, axis, [(low, low ^ apart) for low in range(count)])  17.4 us
    pallas_call x8, Pallas kernels, local(): pl.pallas_call(kernel, in_specs=[IN_SMEM] + [IN_VMEM] * len(operands), ou...  16.8 us
    ppermute x3, starting transfers between devices, shifted(): lax.ppermute(block, 'fsdp', [(place, (place + SIDES * hops) % count) for...  7.2 us
    all_to_all x1, waiting for transfers between devices, along_y(): lax.all_to_all(block, 'fsdp', 0, 0, tiled=True, axis_index_groups=ALONG_Y)  4.72 us
    ppermute x3, waiting for transfers between devices, shifted(): lax.ppermute(block, 'fsdp', [(place, (place + SIDES * hops) % count) for...  4.2 us
    all_to_all x1, starting transfers between devices, along_y(): lax.all_to_all(block, 'fsdp', 0, 0, tiled=True, axis_index_groups=ALONG_Y)  3.52 us
  transfers between devices with their start and end apart: 9, of which 6 were waited for; matrix products, arithmetic and copies ran while one was open for 0% of the time, Pallas kernels for 18%

profile of v3, /device:TPU:1, one launch (start us, length us, event | category | flops | bytes accessed | tf_op | source)
XLA Modules:
  0.0 75.5 jit_solution(18404681128336828564)
XLA Ops:
  1.3 74.2 %conditional.1 = (bf16[1,192,512]{2,1,0:T(8,128)(2,1)}, bf16[1,192,4096]{2,1,0:T(8,128)(2,1)}, f32[1,256,512]{2,1,0:T(8,128)}) conditional(s32[]{:T(128)} %clamp.3, (f32[1,256,512]{2,1,0:T(8,128)}, bf16[1,192,4096]{2,1,0:T(8,128)(2,1)}, bf16[1,192,512]{2,1,0:T(8,128)(2,1)}, (), f32[1]{0:T(128)}, /*index=5*/(), ()) %tuple.34, ...), branch_computations={%region_0.1_spmd, %region_1.2_spmd, %region_2.3_spmd} | conditional | flops 566940008448 | bytes 4481614848 | solution.py:175
  1.5 1.7 %pack.3 = bf16[192,2560]{1,0:T(8,128)(2,1)S(1)} custom-call(s32[3]{0:T(128)S(1)} %pad_add_fusion.spot._, bf16[192,4096]{1,0:T(8,128)(2,1)} %bitcast.31, bf16[192,512]{1,0:T(8,128)(2,1)} %bitcast.40), custom_call_target="tpu_custom_call" | custom-call | flops 1048576 | bytes 1048576 | tf_op jit(solution)/shard_map/cond/branch_0_fun/pack/pallas_call | solution.py:43
  3.1 8.8 %collective-permute-start.1 = (bf16[192,2560]{1,0:T(8,128)(2,1)S(1)}, bf16[192,2560]{1,0:T(8,128)(2,1)S(1)}, u32[]{:S(2)}, u32[]{:S(2)}) collective-permute-start(bf16[192,2560]{1,0:T(8,128)(2,1)S(1)} %pack.3), channel_id=1, source_target_pairs={{0,1},{1,0},{2,3},{3,2},{4,5},{5,4},{6,7},{7,6},{8,9},{9,8},{10,11... | collective-permute-start | bytes 2949128 | tf_op jit(solution)/shard_map/cond/branch_0_fun/ppermute | solution.py:57
  12.0 1.9 %collective-permute-start = (bf16[256,512]{1,0:T(8,128)(2,1)S(1)}, bf16[256,512]{1,0:T(8,128)(2,1)S(1)}, u32[]{:S(2)}, u32[]{:S(2)}) collective-permute-start(bf16[256,512]{1,0:T(8,128)(2,1)S(1)} %bitcast_convert_fusion.half), channel_id=1, source_target_pairs={{0,2},{1,3},{2,0},{3,1},{4,6},{5,7},{6,4},{7,5},{8,10},{9,11},{10,... | collective-permute-start | bytes 786440 | tf_op jit(solution)/shard_map/cond/branch_0_fun/ppermute | solution.py:57
  13.9 0.2 collective-permute-done.1.partner
  14.1 1.8 %gradient_terms.3 = (bf16[4,512,256]{2,1,0:T(8,128)(2,1)S(1)}, bf16[4,512,256]{2,1,0:T(8,128)(2,1)S(1)}) custom-call(s32[3]{0:T(128)S(1)} %pad_add_fusion.spot._, bf16[192,4096]{1,0:T(8,128)(2,1)S(1)} %bitcast.32, bf16[192,512]{1,0:T(8,128)(2,1)S(1)} %bitcast.41, bf16[192,2560]{1,0:T(8,128)(2,1)S(1)} %collective-permute-done.1.partner), custom_call_target="tpu_custom_call" | custom-call | flops 1048576 | bytes 1048576 | tf_op jit(solution)/shard_map/cond/branch_0_fun/gradient_terms/pallas_call | solution.py:43
  15.9 4.7 %collective-permute-start.3 = (bf16[4,512,256]{2,1,0:T(8,128)(2,1)S(1)}, bf16[4,512,256]{2,1,0:T(8,128)(2,1)S(1)}, u32[]{:S(2)}, u32[]{:S(2)}) collective-permute-start(bf16[4,512,256]{2,1,0:T(8,128)(2,1)S(1)} %get-tuple-element.29), channel_id=1, source_target_pairs={{0,2},{1,3},{2,0},{3,1},{4,6},{5,7},{6,4},{7,5},{8,10},{9,11},{10,... | collective-permute-start | bytes 3145736 | tf_op jit(solution)/shard_map/cond/branch_0_fun/ppermute | solution.py:57
  20.7 2.6 %collective-permute-done.near = bf16[256,512]{1,0:T(8,128)(2,1)S(1)} collective-permute-done((bf16[256,512]{1,0:T(8,128)(2,1)S(1)}, bf16[256,512]{1,0:T(8,128)(2,1)S(1)}, u32[]{:S(2)}, u32[]{:S(2)}) %collective-permute-start) | collective-permute-done | bytes 262176 | tf_op jit(solution)/shard_map/cond/branch_0_fun/ppermute | solution.py:57
  23.3 1.4 %pair_up.3.refs_0_ = bf16[2,256,512]{2,1,0:T(8,128)(2,1)} custom-call(s32[3]{0:T(128)S(1)} %pad_add_fusion.spot._, bf16[256,512]{1,0:T(8,128)(2,1)S(1)} %bitcast_convert_fusion.half, bf16[256,512]{1,0:T(8,128)(2,1)S(1)} %collective-permute-done.near), custom_call_target="tpu_custom_call" | custom-call | flops 8589934592 | bytes 67108864 | tf_op jit(solution)/shard_map/cond/branch_0_fun/pair_up/pallas_call | solution.py:43
  24.7 1.9 %collective-permute-start.5 = (bf16[2,256,512]{2,1,0:T(8,128)(2,1)}, bf16[2,256,512]{2,1,0:T(8,128)(2,1)}, u32[]{:S(2)}, u32[]{:S(2)}) collective-permute-start(bf16[2,256,512]{2,1,0:T(8,128)(2,1)} %pair_up.3.refs_0_), channel_id=1, source_target_pairs={{0,12},{1,13},{2,14},{3,15},{4,0},{5,1},{6,2},{7,3},{8,4},{9,5},{1... | collective-permute-start | bytes 1572872 | tf_op jit(solution)/shard_map/cond/branch_0_fun/ppermute | solution.py:66
  26.6 1.9 %collective-permute-start.4 = (bf16[2,256,512]{2,1,0:T(8,128)(2,1)}, bf16[2,256,512]{2,1,0:T(8,128)(2,1)}, u32[]{:S(2)}, u32[]{:S(2)}) collective-permute-start(bf16[2,256,512]{2,1,0:T(8,128)(2,1)} %pair_up.3.refs_0_), channel_id=1, source_target_pairs={{0,8},{1,9},{2,10},{3,11},{4,12},{5,13},{6,14},{7,15},{8,0},{9,1},... | collective-permute-start | bytes 1572872 | tf_op jit(solution)/shard_map/cond/branch_0_fun/ppermute | solution.py:66
  28.5 3.4 %collective-permute-start.2 = (bf16[2,256,512]{2,1,0:T(8,128)(2,1)}, bf16[2,256,512]{2,1,0:T(8,128)(2,1)}, u32[]{:S(2)}, u32[]{:S(2)}) collective-permute-start(bf16[2,256,512]{2,1,0:T(8,128)(2,1)} %pair_up.3.refs_0_), channel_id=1, source_target_pairs={{0,4},{1,5},{2,6},{3,7},{4,8},{5,9},{6,10},{7,11},{8,12},{9,13},{1... | collective-permute-start | bytes 1572872 | tf_op jit(solution)/shard_map/cond/branch_0_fun/ppermute | solution.py:66
  31.9 14.0 %collective-permute-done.3.taken = bf16[4,512,256]{2,1,0:T(8,128)(2,1)S(1)} collective-permute-done((bf16[4,512,256]{2,1,0:T(8,128)(2,1)S(1)}, bf16[4,512,256]{2,1,0:T(8,128)(2,1)S(1)}, u32[]{:S(2)}, u32[]{:S(2)}) %collective-permute-start.3) | collective-permute-done | bytes 1048608 | tf_op jit(solution)/shard_map/cond/branch_0_fun/ppermute | solution.py:57
  45.9 1.7 %fold.3 = bf16[4,512,256]{2,1,0:T(8,128)(2,1)} custom-call(s32[3]{0:T(128)S(1)} %pad_add_fusion.spot._, bf16[4,512,256]{2,1,0:T(8,128)(2,1)S(1)} %get-tuple-element.27.kept, bf16[4,512,256]{2,1,0:T(8,128)(2,1)S(1)} %collective-permute-done.3.taken), custom_call_target="tpu_custom_call" | custom-call | flops 274877906944 | bytes 1048576 | tf_op jit(solution)/shard_map/cond/branch_0_fun/fold/pallas_call | solution.py:43
  47.6 3.5 %all-to-all-start = ((bf16[4,512,256]{2,1,0:T(8,128)(2,1)}), bf16[4,512,256]{2,1,0:T(8,128)(2,1)S(1)}, u32[]{:S(2)}, u32[]{:S(2)}) async-start(bf16[4,512,256]{2,1,0:T(8,128)(2,1)} %fold.3), calls=%async_computation | async-start | bytes 2097152 | tf_op jit(solution)/shard_map/cond/branch_0_fun/all_to_all | solution.py:61
  51.2 4.2 %collective-permute-done.2.refs_1_ = bf16[2,256,512]{2,1,0:T(8,128)(2,1)} collective-permute-done((bf16[2,256,512]{2,1,0:T(8,128)(2,1)}, bf16[2,256,512]{2,1,0:T(8,128)(2,1)}, u32[]{:S(2)}, u32[]{:S(2)}) %collective-permute-start.2) | collective-permute-done | bytes 524320 | tf_op jit(solution)/shard_map/cond/branch_0_fun/ppermute | solution.py:66
  55.4 3.0 %gather.3.mine = bf16[4,2,256,512]{3,2,1,0:T(8,128)(2,1)} custom-call(s32[3]{0:T(128)S(1)} %pad_add_fusion.spot._, bf16[2,256,512]{2,1,0:T(8,128)(2,1)} %pair_up.3.refs_0_, bf16[2,256,512]{2,1,0:T(8,128)(2,1)} %collective-permute-done.2.refs_1_, bf16[2,256,512]{2,1,0:T(8,128)(2,1)} %collective-permute-done.4.refs_2_, ...), custom_call_target="tpu_custom_call" | custom-call | flops 8589934592 | bytes 67108864 | tf_op jit(solution)/shard_map/cond/branch_0_fun/gather/pallas_call | solution.py:43
  58.4 2.5 %collective-permute-start.6 = (bf16[4,2,256,512]{3,2,1,0:T(8,128)(2,1)}, bf16[4,2,256,512]{3,2,1,0:T(8,128)(2,1)}, u32[]{:S(2)}, u32[]{:S(2)}) collective-permute-start(bf16[4,2,256,512]{3,2,1,0:T(8,128)(2,1)} %gather.3.mine), channel_id=1, source_target_pairs={{0,1},{1,0},{2,3},{3,2},{4,5},{5,4},{6,7},{7,6},{8,9},{9,8},{10,11... | collective-permute-start | bytes 6291464 | tf_op jit(solution)/shard_map/cond/branch_0_fun/ppermute | solution.py:57
  60.9 4.7 %all-to-all-done.terms = bf16[4,512,256]{2,1,0:T(8,128)(2,1)S(1)} async-done(((bf16[4,512,256]{2,1,0:T(8,128)(2,1)}), bf16[4,512,256]{2,1,0:T(8,128)(2,1)S(1)}, u32[]{:S(2)}, u32[]{:S(2)}) %all-to-all-start) | async-done | bytes 1048608 | tf_op jit(solution)/shard_map/cond/branch_0_fun/all_to_all | solution.py:61
  65.6 0.2 update.3
  65.8 2.1 %collective-permute-start.7 = (bf16[256,512]{1,0:T(8,128)(2,1)S(1)}, bf16[256,512]{1,0:T(8,128)(2,1)S(1)}, u32[]{:S(2)}, u32[]{:S(2)}) collective-permute-start(bf16[256,512]{1,0:T(8,128)(2,1)S(1)} %get-tuple-element.37), channel_id=1, source_target_pairs={{0,16},{16,0},{32,48},{48,32},{64,80},{80,64},{96,112},{112,96},{1... | collective-permute-start | bytes 786440 | tf_op jit(solution)/shard_map/cond/branch_0_fun/ppermute | solution.py:57
  67.9 5.6 %keys.3 = (bf16[192,512]{1,0:T(8,128)(2,1)}, bf16[192,4096]{1,0:T(8,128)(2,1)}) custom-call(s32[3]{0:T(128)S(1)} %pad_add_fusion.spot._, bf16[192,4096]{1,0:T(8,128)(2,1)S(1)} %bitcast.33, bf16[192,512]{1,0:T(8,128)(2,1)S(1)} %bitcast.42, bf16[4,2,256,512]{3,2,1,0:T(8,128)(2,1)} %gather.3.mine, bf16[4,2,256,512]{3,2,1,0:T(8,128)(2,1)} %collective-permute-done.6.theirs), custom_call_target="tpu_custom_call" | custom-call | flops 1048576 | bytes 1048576 | tf_op jit(solution)/shard_map/cond/branch_0_fun/keys/pallas_call | solution.py:43
  73.5 0.6 collective-permute-done.7.other
  74.1 1.4 %mix.3 = f32[256,512]{1,0:T(8,128)} custom-call(s32[3]{0:T(128)S(1)} %pad_add_fusion.spot._, f32[256,512]{1,0:T(8,128)S(1)} %get-tuple-element.36.updated, bf16[256,512]{1,0:T(8,128)(2,1)S(1)} %collective-permute-done.7.other), custom_call_target="tpu_custom_call" | custom-call | flops 1048576 | bytes 1048576 | tf_op jit(solution)/shard_map/cond/branch_0_fun/mix/pallas_call | solution.py:43
  (17 shorter events, 0.2 us)
Async XLA Ops:
  1.3 10.6 %copy-start.12 = (f32[1,256,512]{2,1,0:T(8,128)S(1)}, f32[1,256,512]{2,1,0:T(8,128)}, u32[]{:S(2)}) copy-start(f32[1,256,512]{2,1,0:T(8,128)} %get-tuple-element.102) | copy-start | bytes 1572868 | tf_op jit(solution)/shard_map/cond
  1.3 12.8 %copy-start = (bf16[1,192,4096]{2,1,0:T(8,128)(2,1)S(1)}, bf16[1,192,4096]{2,1,0:T(8,128)(2,1)}, u32[]{:S(2)}) copy-start(bf16[1,192,4096]{2,1,0:T(8,128)(2,1)} %get-tuple-element.105) | copy-start | bytes 4718596 | tf_op jit(solution)/shard_map/cond
  1.3 12.8 %copy-start.6 = (bf16[1,192,512]{2,1,0:T(8,128)(2,1)S(1)}, bf16[1,192,512]{2,1,0:T(8,128)(2,1)}, u32[]{:S(2)}) copy-start(bf16[1,192,512]{2,1,0:T(8,128)(2,1)} %get-tuple-element.108) | copy-start | bytes 589828 | tf_op jit(solution)/shard_map/cond
  3.1 11.0 %collective-permute-start.1 = (bf16[192,2560]{1,0:T(8,128)(2,1)S(1)}, bf16[192,2560]{1,0:T(8,128)(2,1)S(1)}, u32[]{:S(2)}, u32[]{:S(2)}) collective-permute-start(bf16[192,2560]{1,0:T(8,128)(2,1)S(1)} %pack.3), channel_id=1, source_target_pairs={{0,1},{1,0},{2,3},{3,2},{4,5},{5,4},{6,7},{7,6},{8,9},{9,8},{10,11... | collective-permute-start | bytes 2949128 | tf_op jit(solution)/shard_map/cond/branch_0_fun/ppermute | solution.py:57
  12.0 11.3 %collective-permute-start = (bf16[256,512]{1,0:T(8,128)(2,1)S(1)}, bf16[256,512]{1,0:T(8,128)(2,1)S(1)}, u32[]{:S(2)}, u32[]{:S(2)}) collective-permute-start(bf16[256,512]{1,0:T(8,128)(2,1)S(1)} %bitcast_convert_fusion.half), channel_id=1, source_target_pairs={{0,2},{1,3},{2,0},{3,1},{4,6},{5,7},{6,4},{7,5},{8,10},{9,11},{10,... | collective-permute-start | bytes 786440 | tf_op jit(solution)/shard_map/cond/branch_0_fun/ppermute | solution.py:57
  15.9 29.9 %collective-permute-start.3 = (bf16[4,512,256]{2,1,0:T(8,128)(2,1)S(1)}, bf16[4,512,256]{2,1,0:T(8,128)(2,1)S(1)}, u32[]{:S(2)}, u32[]{:S(2)}) collective-permute-start(bf16[4,512,256]{2,1,0:T(8,128)(2,1)S(1)} %get-tuple-element.29), channel_id=1, source_target_pairs={{0,2},{1,3},{2,0},{3,1},{4,6},{5,7},{6,4},{7,5},{8,10},{9,11},{10,... | collective-permute-start | bytes 3145736 | tf_op jit(solution)/shard_map/cond/branch_0_fun/ppermute | solution.py:57
  24.7 26.5 %collective-permute-start.5 = (bf16[2,256,512]{2,1,0:T(8,128)(2,1)}, bf16[2,256,512]{2,1,0:T(8,128)(2,1)}, u32[]{:S(2)}, u32[]{:S(2)}) collective-permute-start(bf16[2,256,512]{2,1,0:T(8,128)(2,1)} %pair_up.3.refs_0_), channel_id=1, source_target_pairs={{0,12},{1,13},{2,14},{3,15},{4,0},{5,1},{6,2},{7,3},{8,4},{9,5},{1... | collective-permute-start | bytes 1572872 | tf_op jit(solution)/shard_map/cond/branch_0_fun/ppermute | solution.py:66
  26.6 24.6 %collective-permute-start.4 = (bf16[2,256,512]{2,1,0:T(8,128)(2,1)}, bf16[2,256,512]{2,1,0:T(8,128)(2,1)}, u32[]{:S(2)}, u32[]{:S(2)}) collective-permute-start(bf16[2,256,512]{2,1,0:T(8,128)(2,1)} %pair_up.3.refs_0_), channel_id=1, source_target_pairs={{0,8},{1,9},{2,10},{3,11},{4,12},{5,13},{6,14},{7,15},{8,0},{9,1},... | collective-permute-start | bytes 1572872 | tf_op jit(solution)/shard_map/cond/branch_0_fun/ppermute | solution.py:66
  28.5 26.9 %collective-permute-start.2 = (bf16[2,256,512]{2,1,0:T(8,128)(2,1)}, bf16[2,256,512]{2,1,0:T(8,128)(2,1)}, u32[]{:S(2)}, u32[]{:S(2)}) collective-permute-start(bf16[2,256,512]{2,1,0:T(8,128)(2,1)} %pair_up.3.refs_0_), channel_id=1, source_target_pairs={{0,4},{1,5},{2,6},{3,7},{4,8},{5,9},{6,10},{7,11},{8,12},{9,13},{1... | collective-permute-start | bytes 1572872 | tf_op jit(solution)/shard_map/cond/branch_0_fun/ppermute | solution.py:66
  47.6 18.0 %all-to-all-start = ((bf16[4,512,256]{2,1,0:T(8,128)(2,1)}), bf16[4,512,256]{2,1,0:T(8,128)(2,1)S(1)}, u32[]{:S(2)}, u32[]{:S(2)}) async-start(bf16[4,512,256]{2,1,0:T(8,128)(2,1)} %fold.3), calls=%async_computation | async-start | bytes 2097152 | tf_op jit(solution)/shard_map/cond/branch_0_fun/all_to_all | solution.py:61
  51.2 14.5 %copy-start.13 = (f32[1,256,512]{2,1,0:T(8,128)S(1)}, f32[1,256,512]{2,1,0:T(8,128)}, u32[]{:S(2)}) copy-start(f32[1,256,512]{2,1,0:T(8,128)} %get-tuple-element.102) | copy-start | bytes 1572868 | tf_op jit(solution)/shard_map/cond
  58.4 9.5 %collective-permute-start.6 = (bf16[4,2,256,512]{3,2,1,0:T(8,128)(2,1)}, bf16[4,2,256,512]{3,2,1,0:T(8,128)(2,1)}, u32[]{:S(2)}, u32[]{:S(2)}) collective-permute-start(bf16[4,2,256,512]{3,2,1,0:T(8,128)(2,1)} %gather.3.mine), channel_id=1, source_target_pairs={{0,1},{1,0},{2,3},{3,2},{4,5},{5,4},{6,7},{7,6},{8,9},{9,8},{10,11... | collective-permute-start | bytes 6291464 | tf_op jit(solution)/shard_map/cond/branch_0_fun/ppermute | solution.py:57
  65.6 2.3 %copy-start.1 = (bf16[1,192,4096]{2,1,0:T(8,128)(2,1)S(1)}, bf16[1,192,4096]{2,1,0:T(8,128)(2,1)}, u32[]{:S(2)}) copy-start(bf16[1,192,4096]{2,1,0:T(8,128)(2,1)} %get-tuple-element.105) | copy-start | bytes 4718596 | tf_op jit(solution)/shard_map/cond
  65.6 2.3 %copy-start.7 = (bf16[1,192,512]{2,1,0:T(8,128)(2,1)S(1)}, bf16[1,192,512]{2,1,0:T(8,128)(2,1)}, u32[]{:S(2)}) copy-start(bf16[1,192,512]{2,1,0:T(8,128)(2,1)} %get-tuple-element.108) | copy-start | bytes 589828 | tf_op jit(solution)/shard_map/cond
  65.8 8.3 %collective-permute-start.7 = (bf16[256,512]{1,0:T(8,128)(2,1)S(1)}, bf16[256,512]{1,0:T(8,128)(2,1)S(1)}, u32[]{:S(2)}, u32[]{:S(2)}) collective-permute-start(bf16[256,512]{1,0:T(8,128)(2,1)S(1)} %get-tuple-element.37), channel_id=1, source_target_pairs={{0,16},{16,0},{32,48},{48,32},{64,80},{80,64},{96,112},{112,96},{1... | collective-permute-start | bytes 786440 | tf_op jit(solution)/shard_map/cond/branch_0_fun/ppermute | solution.py:57
